TPU v7x, 256 devices: a whole 4x4x8 slice. The times are simulated.
256 devices in a mesh: gx: 32 (over y_lo, z, core), gy: 8 (over x, y_hi).
Axes of the slice: x: 4, y: 4 (y_hi: 2, y_lo: 2; y = y_hi * 2 + y_lo), z: 8, core: 2. Of those that a mesh axis runs over, the one named last changes fastest.
Arguments:
- occupancy: int32 [2, 1024, 1024], P(None, 'gx', 'gy'), may hold values from 0 to 1, as said below
- colour: int32 [2, 1024, 1024], P(None, 'gx', 'gy'), may hold values 0 or 1
- hop_direction: int32 [2, 2, 1024, 1024], P(None, None, 'gx', 'gy'), may hold values from 0 to 3
- barrier: float32 [2, 1024, 1024], P(None, 'gx', 'gy'), may hold values from -4 to 4
Outputs:
- strain: float32 [3, 2, 1024, 1024], P(None, None, 'gx', 'gy')
- composition: float32 [2, 1024, 1024], P(None, 'gx', 'gy')
Inputs may be any that keep to these rules, and one draw needn't show every extreme that they name: `occupancy`: 1 for a Ge atom, 0 for Si.
All inputs are finite; a program needn't handle non-finite values. No bound on the sum of `colour` on one device may be relied on, other than what follows from the above.
Results may differ from a plain program's by a relative error of at most 0.00011.
Values sent between devices are 32-bit elements; how exact they have to be, the bound alone decides.
A program may use at most 128 MiB of HBM per device.

v0:
```python
import math

import jax
import jax.numpy as jnp
from jax import lax
from jax.sharding import PartitionSpec as P

ITERS = 3
SECTIONS = 2


lame_silicon = 1.2
lame_germanium = 0.9
shear_silicon = 1.0
shear_germanium = 0.8
lame_medium = 1.05
shear_medium = 0.9
elastic_weight = 2.0
bond_energy = 0.7
base_rate = 1.0


def padded(cells, sides, width):
    for axis, dim in sides:
        count = lax.axis_size(axis)
        head = lax.slice_in_dim(cells, 0, width, axis=dim)
        tail = lax.slice_in_dim(cells, cells.shape[dim] - width, cells.shape[dim], axis=dim)
        cells = jnp.concatenate(
            [
                lax.ppermute(tail, axis, [(i, (i + 1) % count) for i in range(count)]),
                cells,
                lax.ppermute(head, axis, [((i + 1) % count, i) for i in range(count)]),
            ],
            axis=dim,
        )
    return cells


def local_stress(strain, fraction):
    lame_field = lame_silicon + (lame_germanium - lame_silicon) * fraction
    shear_field = shear_silicon + (shear_germanium - shear_silicon) * fraction
    excess_xx = strain[0] - fraction
    excess_yy = strain[1] - fraction
    trace_part = lame_field * (excess_xx + excess_yy)
    return jnp.stack(
        [
            trace_part + 2.0 * shear_field * excess_xx,
            trace_part + 2.0 * shear_field * excess_yy,
            2.0 * shear_field * strain[2],
        ]
    )


def energy_density(strain, fraction):
    stress = local_stress(strain, fraction)
    return 0.5 * (
        stress[0] * (strain[0] - fraction)
        + stress[1] * (strain[1] - fraction)
        + 2.0 * stress[2] * strain[2]
    )


def wave_numbers(points, first_index, length_of):
    index = first_index + jnp.arange(length_of, dtype=jnp.int32)
    signed = jnp.where(index < points // 2, index, index - points)
    return signed.astype(jnp.float32) * (2.0 * math.pi / points)


def green_apply(part_xx, part_yy, part_xy, wave_x, wave_y):
    ratio = (lame_medium + shear_medium) / (lame_medium + 2.0 * shear_medium)
    squared = wave_x * wave_x + wave_y * wave_y
    positive = squared > 0
    inverse_sq = jnp.where(positive, 1.0 / jnp.where(positive, squared, 1.0), 0.0)
    trac_x = wave_x * part_xx + wave_y * part_xy
    trac_y = wave_x * part_xy + wave_y * part_yy
    along = ratio * (wave_x * trac_x + wave_y * trac_y) * inverse_sq
    disp_x = (trac_x - wave_x * along) * inverse_sq / shear_medium
    disp_y = (trac_y - wave_y * along) * inverse_sq / shear_medium
    return jnp.stack([wave_x * disp_x, wave_y * disp_y, 0.5 * (wave_x * disp_y + wave_y * disp_x)])


def dft_tables(points):
    index = jnp.arange(points, dtype=jnp.int32)
    product = index[:, None] * index[None, :] % points
    angle = product.astype(jnp.float32) * (2.0 * math.pi / points)
    return (jnp.cos(angle), jnp.sin(angle))


def twiddle_tables(outer, inner):
    points = outer * inner
    first = jnp.arange(outer, dtype=jnp.int32)[:, None]
    second = jnp.arange(inner, dtype=jnp.int32)[None, :]
    angle = (first * second % points).astype(jnp.float32) * (2.0 * math.pi / points)
    return (jnp.cos(angle), jnp.sin(angle))


def contract(form, left, right):
    return jnp.einsum(
        form, left, right, precision=lax.Precision.HIGHEST, preferred_element_type=jnp.float32
    )


def dft_last(real_part, imag_part, sign, real_only):
    points = real_part.shape[-1]
    half_bits = (points.bit_length() - 1) // 2
    outer = 2**half_bits
    inner = points // outer
    lead = real_part.shape[:-1]
    outer_cos, outer_sin = dft_tables(outer)
    inner_cos, inner_sin = dft_tables(inner)
    turn_cos, turn_sin = twiddle_tables(outer, inner)
    outer_sin = sign * outer_sin
    inner_sin = sign * inner_sin
    turn_sin = sign * turn_sin
    shaped_real = real_part.reshape(lead + (outer, inner))
    first_real = contract("...jt,jk->...kt", shaped_real, outer_cos)
    first_imag = contract("...jt,jk->...kt", shaped_real, outer_sin)
    if imag_part is not None:
        shaped_imag = imag_part.reshape(lead + (outer, inner))
        first_real = first_real - contract("...jt,jk->...kt", shaped_imag, outer_sin)
        first_imag = first_imag + contract("...jt,jk->...kt", shaped_imag, outer_cos)
    turned_real = first_real * turn_cos - first_imag * turn_sin
    turned_imag = first_real * turn_sin + first_imag * turn_cos
    final_real = contract("...kt,tm->...mk", turned_real, inner_cos) - contract(
        "...kt,tm->...mk", turned_imag, inner_sin
    )
    if real_only:
        return (final_real.reshape(lead + (points,)), None)
    final_imag = contract("...kt,tm->...mk", turned_real, inner_sin) + contract(
        "...kt,tm->...mk", turned_imag, inner_cos
    )
    return (final_real.reshape(lead + (points,)), final_imag.reshape(lead + (points,)))


def hop_flux(
    composition, above, below, before, after, energy, barrier, colour, direction, section_index
):
    neighbours = above + below + before + after
    rate = jax.nn.sigmoid(barrier + elastic_weight * energy - bond_energy * neighbours + base_rate)
    target = jnp.where(
        direction == 0,
        below,
        jnp.where(direction == 1, above, jnp.where(direction == 2, after, before)),
    )
    flux = jnp.where(colour == section_index, rate * composition * (1.0 - target), 0.0)
    return (flux, [jnp.where(direction == number, flux, 0.0) for number in range(4)])


def on_device(occupancy, colour, hop_direction, barrier):
    fraction = occupancy.astype(jnp.float32)
    layer_count, rows_x, cols_y = fraction.shape
    groups_y = lax.axis_size("gy")
    groups_x = lax.axis_size("gx")
    row_share = rows_x // groups_y
    spectral_rows = cols_y // groups_x
    total_x = rows_x * groups_x
    total_y = cols_y * groups_y
    wave_x = wave_numbers(total_x, 0, total_x)[None, :]
    first_freq = lax.axis_index("gy") * cols_y + lax.axis_index("gx") * spectral_rows
    wave_y = wave_numbers(total_y, first_freq, spectral_rows)[:, None]
    scale = 1.0 / (total_x * total_y)

    def relay_rows(values_in):
        return lax.all_to_all(values_in, "gy", split_axis=1, concat_axis=1, tiled=True)

    def relay_spectrum(values_in):
        return lax.all_to_all(
            lax.all_to_all(values_in, "gx", split_axis=4, concat_axis=4, tiled=True),
            "gy",
            split_axis=3,
            concat_axis=3,
            tiled=True,
        )

    def apply_layers(spectral_field, first):
        if first:
            shaped = spectral_field
            mapped = green_apply(shaped, shaped, jnp.zeros_like(shaped), wave_x, wave_y) * scale
        else:
            shaped = spectral_field.reshape(3, layer_count, spectral_rows, total_x)
            mapped = green_apply(shaped[0], shaped[1], shaped[2], wave_x, wave_y) * scale
        return mapped.reshape(3 * layer_count, spectral_rows, total_x)

    def correction(pencil_field, first):
        merged = pencil_field.shape[0]
        real_y, imag_y = dft_last(pencil_field, None, -1.0, False)
        joined = jnp.stack([real_y, imag_y]).reshape(
            2, merged, row_share, groups_y, groups_x, spectral_rows
        )
        mixed = relay_spectrum(joined)
        spectral = mixed.transpose(0, 1, 5, 4, 3, 2).reshape(2, merged, spectral_rows, total_x)
        real_x, imag_x = dft_last(spectral[0], spectral[1], -1.0, False)
        green_real = apply_layers(real_x, first)
        green_imag = apply_layers(imag_x, first)
        back_real, back_imag = dft_last(green_real, green_imag, 1.0, False)
        outgoing = (
            jnp.stack([back_real, back_imag])
            .reshape(2, 3 * layer_count, spectral_rows, groups_x, groups_y, row_share)
            .transpose(0, 1, 5, 4, 3, 2)
        )
        returned = relay_spectrum(outgoing).reshape(2, 3 * layer_count, row_share, total_y)
        result, unused = dft_last(returned[0], returned[1], 1.0, True)
        return result

    number = fraction.shape[0]
    moved = relay_rows(fraction.reshape(number, groups_y, row_share, cols_y))
    fraction_pencil = moved.transpose(0, 2, 1, 3).reshape(number, row_share, total_y)
    strain_pencil = jnp.zeros((3, layer_count, row_share, total_y), jnp.float32)
    for sweep_index in range(ITERS):
        stress = local_stress(strain_pencil, fraction_pencil)
        if sweep_index == 0:
            change = correction(stress[0], True)
        else:
            change = correction(stress.reshape(3 * layer_count, row_share, total_y), False)
        strain_pencil = strain_pencil - change.reshape(3, layer_count, row_share, total_y)
    pencil_field = strain_pencil.reshape(3 * layer_count, row_share, total_y)
    number = pencil_field.shape[0]
    shaped = pencil_field.reshape(number, row_share, groups_y, cols_y).transpose(0, 2, 1, 3)
    moved = relay_rows(shaped)
    strain = moved.reshape(number, rows_x, cols_y)
    strain = strain.reshape(3, layer_count, rows_x, cols_y)
    energy = energy_density(strain, fraction)
    composition = fraction
    for section_index in range(SECTIONS):
        extended = padded(composition, (("gx", 1), ("gy", 2)), 1)
        above = extended[:, :-2, 1:-1]
        below = extended[:, 2:, 1:-1]
        before = extended[:, 1:-1, :-2]
        after = extended[:, 1:-1, 2:]
        flux, parted = hop_flux(
            composition,
            above,
            below,
            before,
            after,
            energy,
            barrier,
            colour,
            hop_direction[section_index],
            section_index,
        )
        edge_rows = jnp.stack([parted[1][:, 0], parted[0][:, -1]])
        rows_ext = padded(edge_rows, (("gx", 0),), 1)
        edge_cols = jnp.stack([parted[3][:, :, 0], parted[2][:, :, -1]])
        cols_ext = padded(edge_cols, (("gy", 0),), 1)
        from_above = jnp.concatenate([rows_ext[0][:, None, :], parted[0][:, :-1]], axis=1)
        from_below = jnp.concatenate([parted[1][:, 1:], rows_ext[3][:, None, :]], axis=1)
        from_before = jnp.concatenate([cols_ext[0][:, :, None], parted[2][:, :, :-1]], axis=2)
        from_after = jnp.concatenate([parted[3][:, :, 1:], cols_ext[3][:, :, None]], axis=2)
        composition = composition - flux + (from_above + from_below + from_before + from_after)
    return (strain, composition)


def solution(mesh):
    placed = (
        P(None, "gx", "gy"),
        P(None, "gx", "gy"),
        P(None, None, "gx", "gy"),
        P(None, "gx", "gy"),
    )
    return jax.shard_map(
        on_device,
        mesh=mesh,
        in_specs=placed,
        out_specs=(P(None, None, "gx", "gy"), P(None, "gx", "gy")),
        check_vma=False,
    )
```

profile of v0, /device:TPU:1, one launch (start us, length us, event | category | flops | bytes accessed | tf_op | source)
XLA Modules:
  0.0 542.5 jit_solution(8528759003531568105)
XLA Ops:
  2.0 7.5 %all-to-all-start = ((f32[2,8,4,128]{3,2,0,1:T(4,128)}), f32[2,8,4,128]{3,2,0,1:T(4,128)S(1)}, u32[]{:S(2)}, u32[]{:S(2)}) async-start(f32[2,8,4,128]{3,2,0,1:T(4,128)} %copy.766), calls=%async_computation | async-start | bytes 65536 | tf_op jit(solution)/shard_map/all_to_all | solution.py:164
  10.0 6.1 %all-to-all-done = f32[2,8,4,128]{3,2,0,1:T(4,128)S(1)} async-done(((f32[2,8,4,128]{3,2,0,1:T(4,128)}), f32[2,8,4,128]{3,2,0,1:T(4,128)S(1)}, u32[]{:S(2)}, u32[]{:S(2)}) %all-to-all-start) | async-done | bytes 32800 | tf_op jit(solution)/shard_map/all_to_all | solution.py:164
  28.2 10.8 %all-to-all-start.1 = ((f32[32,1,512]{2,1,0:T(1,128)}), f32[32,1,512]{2,1,0:T(1,128)S(1)}, u32[]{:S(2)}, u32[]{:S(2)}) async-start(f32[32,1,512]{2,1,0:T(1,128)} %reshape.1002), calls=%async_computation.1 | async-start | bytes 131072 | tf_op jit(solution)/shard_map/all_to_all | solution.py:168
  39.1 8.0 %all-to-all-done.1 = f32[32,1,512]{2,1,0:T(1,128)S(1)} async-done(((f32[32,1,512]{2,1,0:T(1,128)}), f32[32,1,512]{2,1,0:T(1,128)S(1)}, u32[]{:S(2)}, u32[]{:S(2)}) %all-to-all-start.1) | async-done | bytes 65568 | tf_op jit(solution)/shard_map/all_to_all | solution.py:168
  55.2 6.5 %all-to-all-done.2 = f32[8,1,2048]{2,1,0:T(1,128)S(1)} async-done(((f32[8,1,2048]{2,1,0:T(1,128)}), f32[8,1,2048]{2,1,0:T(1,128)S(1)}, u32[]{:S(2)}, u32[]{:S(2)}) %all-to-all-start.2) | async-done | bytes 65568 | tf_op jit(solution)/shard_map/all_to_all | solution.py:167
  81.1 4.9 copy.782
  89.6 15.3 %all_to_all.70 = f32[32,1,1536]{2,1,0:T(1,128)S(1)} all-to-all(f32[32,1,1536]{2,1,0:T(1,128)S(1)} %reshape.1006), channel_id=1, replica_groups=mesh['gx'=32,'gy'=8] {'gx'}, dimensions={0} | all-to-all | bytes 393216 | tf_op jit(solution)/shard_map/all_to_all | solution.py:168
  118.6 7.0 %all-to-all-done.4 = f32[8,1,6144]{2,1,0:T(1,128)S(1)} async-done(((f32[8,1,6144]{2,1,0:T(1,128)}), f32[8,1,6144]{2,1,0:T(1,128)S(1)}, u32[]{:S(2)}, u32[]{:S(2)}) %all-to-all-start.4) | async-done | bytes 196640 | tf_op jit(solution)/shard_map/all_to_all | solution.py:167
  166.5 5.6 %pad_maximum_fusion = f32[2,6,4,8,32,4]{5,4,3,2,1,0:T(8,128)} fusion(f32[1,6,4,8,32,4]{5,4,3,2,1,0:T(8,128)} %stack.100, f32[1,6,4,8,32,4]{5,4,3,2,1,0:T(8,128)S(1)} %stack.99), kind=kLoop, calls=%fused_computation | loop fusion | flops 49152 | bytes 393216 | tf_op jit(solution)/shard_map/stack | solution.py:187
  172.1 11.0 %copy.787 = f32[2,6,4,8,32,4]{3,5,2,1,0,4:T(4,128)S(1)} copy(f32[2,6,4,8,32,4]{5,4,3,2,1,0:T(8,128)} %pad_maximum_fusion) | data formatting | bytes 393216 | tf_op jit(solution)/shard_map/stack | solution.py:187
  186.8 15.8 %all_to_all.71 = f32[32,1,1536]{2,1,0:T(1,128)S(1)} all-to-all(f32[32,1,1536]{2,1,0:T(1,128)S(1)} %reshape.1010), channel_id=1, replica_groups=mesh['gx'=32,'gy'=8] {'gx'}, dimensions={0} | all-to-all | bytes 393216 | tf_op jit(solution)/shard_map/all_to_all | solution.py:168
  211.9 9.5 %all_to_all.72 = f32[8,1,6144]{2,1,0:T(1,128)S(1)} all-to-all(f32[8,1,6144]{2,1,0:T(1,128)S(1)} %reshape.1012), channel_id=1, replica_groups=mesh['gx'=32,'gy'=8] {'gy'}, dimensions={0} | all-to-all | bytes 393216 | tf_op jit(solution)/shard_map/all_to_all | solution.py:167
  259.8 16.2 %all_to_all.73 = f32[32,1,1536]{2,1,0:T(1,128)S(1)} all-to-all(f32[32,1,1536]{2,1,0:T(1,128)S(1)} %reshape.1014), channel_id=1, replica_groups=mesh['gx'=32,'gy'=8] {'gx'}, dimensions={0} | all-to-all | bytes 393216 | tf_op jit(solution)/shard_map/all_to_all | solution.py:168
  285.3 9.8 %all_to_all.74 = f32[8,1,6144]{2,1,0:T(1,128)S(1)} all-to-all(f32[8,1,6144]{2,1,0:T(1,128)S(1)} %reshape.1016), channel_id=1, replica_groups=mesh['gx'=32,'gy'=8] {'gy'}, dimensions={0} | all-to-all | bytes 393216 | tf_op jit(solution)/shard_map/all_to_all | solution.py:167
  336.2 5.6 %pad_maximum_fusion.1 = f32[2,6,4,8,32,4]{5,4,3,2,1,0:T(8,128)} fusion(f32[1,6,4,8,32,4]{5,4,3,2,1,0:T(8,128)} %stack.109, f32[1,6,4,8,32,4]{5,4,3,2,1,0:T(8,128)S(1)} %stack.108), kind=kLoop, calls=%fused_computation.1 | loop fusion | flops 49152 | bytes 393216 | tf_op jit(solution)/shard_map/stack | solution.py:187
  341.9 11.0 %copy.801 = f32[2,6,4,8,32,4]{3,5,2,1,0,4:T(4,128)S(1)} copy(f32[2,6,4,8,32,4]{5,4,3,2,1,0:T(8,128)} %pad_maximum_fusion.1) | data formatting | bytes 393216 | tf_op jit(solution)/shard_map/stack | solution.py:187
  356.5 16.2 %all_to_all.75 = f32[32,1,1536]{2,1,0:T(1,128)S(1)} all-to-all(f32[32,1,1536]{2,1,0:T(1,128)S(1)} %reshape.1018), channel_id=1, replica_groups=mesh['gx'=32,'gy'=8] {'gx'}, dimensions={0} | all-to-all | bytes 393216 | tf_op jit(solution)/shard_map/all_to_all | solution.py:168
  386.3 6.8 %all-to-all-done.10 = f32[8,1,6144]{2,1,0:T(1,128)S(1)} async-done(((f32[8,1,6144]{2,1,0:T(1,128)}), f32[8,1,6144]{2,1,0:T(1,128)S(1)}, u32[]{:S(2)}, u32[]{:S(2)}) %all-to-all-start.10) | async-done | bytes 196640 | tf_op jit(solution)/shard_map/all_to_all | solution.py:167
  423.5 4.4 copy.811
  432.2 6.4 %all-to-all-start.11 = ((f32[32,1,1536]{2,1,0:T(1,128)}), f32[32,1,1536]{2,1,0:T(1,128)S(1)}, u32[]{:S(2)}, u32[]{:S(2)}) async-start(f32[32,1,1536]{2,1,0:T(1,128)} %reshape.1022), calls=%async_computation.11 | async-start | bytes 393216 | tf_op jit(solution)/shard_map/all_to_all | solution.py:168
  441.1 7.9 %all-to-all-done.11 = f32[32,1,1536]{2,1,0:T(1,128)S(1)} async-done(((f32[32,1,1536]{2,1,0:T(1,128)}), f32[32,1,1536]{2,1,0:T(1,128)S(1)}, u32[]{:S(2)}, u32[]{:S(2)}) %all-to-all-start.11) | async-done | bytes 196640 | tf_op jit(solution)/shard_map/all_to_all | solution.py:168
  462.8 7.0 %all-to-all-done.12 = f32[8,1,6144]{2,1,0:T(1,128)S(1)} async-done(((f32[8,1,6144]{2,1,0:T(1,128)}), f32[8,1,6144]{2,1,0:T(1,128)S(1)}, u32[]{:S(2)}, u32[]{:S(2)}) %all-to-all-start.12) | async-done | bytes 196640 | tf_op jit(solution)/shard_map/all_to_all | solution.py:167
  504.2 4.6 collective-permute-start.4
  536.3 4.5 collective-permute-start.13
  (354 shorter events, 331.5 us)
Async XLA Ops:
  2.0 14.1 %all-to-all-start = ((f32[2,8,4,128]{3,2,0,1:T(4,128)}), f32[2,8,4,128]{3,2,0,1:T(4,128)S(1)}, u32[]{:S(2)}, u32[]{:S(2)}) async-start(f32[2,8,4,128]{3,2,0,1:T(4,128)} %copy.766), calls=%async_computation | async-start | bytes 65536 | tf_op jit(solution)/shard_map/all_to_all | solution.py:164
  28.2 18.9 %all-to-all-start.1 = ((f32[32,1,512]{2,1,0:T(1,128)}), f32[32,1,512]{2,1,0:T(1,128)S(1)}, u32[]{:S(2)}, u32[]{:S(2)}) async-start(f32[32,1,512]{2,1,0:T(1,128)} %reshape.1002), calls=%async_computation.1 | async-start | bytes 131072 | tf_op jit(solution)/shard_map/all_to_all | solution.py:168
  51.5 10.2 %all-to-all-start.2 = ((f32[8,1,2048]{2,1,0:T(1,128)}), f32[8,1,2048]{2,1,0:T(1,128)S(1)}, u32[]{:S(2)}, u32[]{:S(2)}) async-start(f32[8,1,2048]{2,1,0:T(1,128)} %reshape.1004), calls=%async_computation.2 | async-start | bytes 131072 | tf_op jit(solution)/shard_map/all_to_all | solution.py:167
  115.0 10.6 %all-to-all-start.4 = ((f32[8,1,6144]{2,1,0:T(1,128)}), f32[8,1,6144]{2,1,0:T(1,128)S(1)}, u32[]{:S(2)}, u32[]{:S(2)}) async-start(f32[8,1,6144]{2,1,0:T(1,128)} %reshape.1008), calls=%async_computation.4 | async-start | bytes 393216 | tf_op jit(solution)/shard_map/all_to_all | solution.py:167
  382.7 10.5 %all-to-all-start.10 = ((f32[8,1,6144]{2,1,0:T(1,128)}), f32[8,1,6144]{2,1,0:T(1,128)S(1)}, u32[]{:S(2)}, u32[]{:S(2)}) async-start(f32[8,1,6144]{2,1,0:T(1,128)} %reshape.1020), calls=%async_computation.10 | async-start | bytes 393216 | tf_op jit(solution)/shard_map/all_to_all | solution.py:167
  432.2 16.7 %all-to-all-start.11 = ((f32[32,1,1536]{2,1,0:T(1,128)}), f32[32,1,1536]{2,1,0:T(1,128)S(1)}, u32[]{:S(2)}, u32[]{:S(2)}) async-start(f32[32,1,1536]{2,1,0:T(1,128)} %reshape.1022), calls=%async_computation.11 | async-start | bytes 393216 | tf_op jit(solution)/shard_map/all_to_all | solution.py:168
  438.7 2.4 collective-permute-start
  440.4 22.4 %collective-permute-start.1 = (f32[2,1,128]{2,0,1:T(2,128)S(1)}, f32[2,1,128]{2,0,1:T(2,128)S(1)}, u32[]{:S(2)}, u32[]{:S(2)}) collective-permute-start(f32[2,1,128]{2,0,1:T(2,128)S(1)} %get-tuple-element.106), channel_id=1, source_target_pairs={{8,0},{16,8},{24,16},{32,24},{40,32},{48,40},{56,48},{64,56},{72,6... | collective-permute-start | bytes 3080 | tf_op jit(solution)/shard_map/ppermute | solution.py:32
  459.3 10.5 %all-to-all-start.12 = ((f32[8,1,6144]{2,1,0:T(1,128)}), f32[8,1,6144]{2,1,0:T(1,128)S(1)}, u32[]{:S(2)}, u32[]{:S(2)}) async-start(f32[8,1,6144]{2,1,0:T(1,128)} %reshape.1024), calls=%async_computation.12 | async-start | bytes 393216 | tf_op jit(solution)/shard_map/all_to_all | solution.py:167
  492.6 10.1 %all-to-all-start.13 = ((f32[6,8,4,128]{3,2,0,1:T(4,128)}), f32[6,8,4,128]{3,2,0,1:T(4,128)S(1)}, u32[]{:S(2)}, u32[]{:S(2)}) async-start(f32[6,8,4,128]{3,2,0,1:T(4,128)} %bitcast.576), calls=%async_computation.13 | async-start | bytes 196608 | tf_op jit(solution)/shard_map/all_to_all | solution.py:164
  496.1 7.1 %collective-permute-start.2 = (f32[2,34,1]{2,0,1:T(2,128)S(1)}, f32[2,34,1]{2,0,1:T(2,128)S(1)}, u32[]{:S(2)}, u32[]{:S(2)}) collective-permute-start(f32[2,34,1]{2,0,1:T(2,128)S(1)} %get-tuple-element.100), channel_id=1, source_target_pairs={{0,1},{1,2},{2,3},{3,4},{4,5},{5,6},{6,7},{7,0},{8,9},{9,10},{10,1... | collective-permute-start | bytes 824 | tf_op jit(solution)/shard_map/ppermute | solution.py:30
  499.0 4.7 collective-permute-start.3
  504.2 11.2 %collective-permute-start.4 = (f32[1,2,128]{2,1,0:T(2,128)S(1)}, f32[1,2,128]{2,1,0:T(2,128)S(1)}, u32[]{:S(2)}, u32[]{:S(2)}) collective-permute-start(f32[1,2,128]{2,1,0:T(2,128)S(1)} %slice_bitcast_fusion.3), channel_id=1, source_target_pairs={{0,8},{8,16},{16,24},{24,32},{32,40},{40,48},{48,56},{56,64},{64,7... | collective-permute-start | bytes 3080 | tf_op jit(solution)/shard_map/ppermute | solution.py:30
  508.7 6.6 %collective-permute-start.5 = (f32[1,2,128]{2,1,0:T(2,128)S(1)}, f32[1,2,128]{2,1,0:T(2,128)S(1)}, u32[]{:S(2)}, u32[]{:S(2)}) collective-permute-start(f32[1,2,128]{2,1,0:T(2,128)S(1)} %slice_bitcast_fusion.2), channel_id=1, source_target_pairs={{8,0},{16,8},{24,16},{32,24},{40,32},{48,40},{56,48},{64,56},{72,6... | collective-permute-start | bytes 3080 | tf_op jit(solution)/shard_map/ppermute | solution.py:32
  509.1 6.0 %collective-permute-start.6 = (f32[1,2,32]{2,1,0:T(2,128)S(1)}, f32[1,2,32]{2,1,0:T(2,128)S(1)}, u32[]{:S(2)}, u32[]{:S(2)}) collective-permute-start(f32[1,2,32]{2,1,0:T(2,128)S(1)} %bitcast.638), channel_id=1, source_target_pairs={{0,1},{1,2},{2,3},{3,4},{4,5},{5,6},{6,7},{7,0},{8,9},{9,10},{10,1... | collective-permute-start | bytes 776 | tf_op jit(solution)/shard_map/ppermute | solution.py:30
  511.3 4.0 collective-permute-start.7
  515.6 5.6 %collective-permute-start.8 = (f32[2,1,128]{2,0,1:T(2,128)S(1)}, f32[2,1,128]{2,0,1:T(2,128)S(1)}, u32[]{:S(2)}, u32[]{:S(2)}) collective-permute-start(f32[2,1,128]{2,0,1:T(2,128)S(1)} %get-tuple-element.105), channel_id=1, source_target_pairs={{0,8},{8,16},{16,24},{24,32},{32,40},{40,48},{48,56},{56,64},{64,7... | collective-permute-start | bytes 3080 | tf_op jit(solution)/shard_map/ppermute | solution.py:30
  518.8 3.0 collective-permute-start.9
  521.9 6.5 %collective-permute-start.10 = (f32[2,34,1]{2,0,1:T(2,128)S(1)}, f32[2,34,1]{2,0,1:T(2,128)S(1)}, u32[]{:S(2)}, u32[]{:S(2)}) collective-permute-start(f32[2,34,1]{2,0,1:T(2,128)S(1)} %get-tuple-element.98), channel_id=1, source_target_pairs={{0,1},{1,2},{2,3},{3,4},{4,5},{5,6},{6,7},{7,0},{8,9},{9,10},{10,1... | collective-permute-start | bytes 824 | tf_op jit(solution)/shard_map/ppermute | solution.py:30
  524.7 4.3 collective-permute-start.11
  529.4 11.6 %collective-permute-start.12 = (f32[1,2,128]{2,1,0:T(2,128)S(1)}, f32[1,2,128]{2,1,0:T(2,128)S(1)}, u32[]{:S(2)}, u32[]{:S(2)}) collective-permute-start(f32[1,2,128]{2,1,0:T(2,128)S(1)} %slice_bitcast_fusion.1), channel_id=1, source_target_pairs={{0,8},{8,16},{16,24},{24,32},{32,40},{40,48},{48,56},{56,64},{64,7... | collective-permute-start | bytes 3080 | tf_op jit(solution)/shard_map/ppermute | solution.py:30
  531.1 9.7 %collective-permute-start.14 = (f32[1,2,32]{2,1,0:T(2,128)S(1)}, f32[1,2,32]{2,1,0:T(2,128)S(1)}, u32[]{:S(2)}, u32[]{:S(2)}) collective-permute-start(f32[1,2,32]{2,1,0:T(2,128)S(1)} %bitcast.635), channel_id=1, source_target_pairs={{0,1},{1,2},{2,3},{3,4},{4,5},{5,6},{6,7},{7,0},{8,9},{9,10},{10,1... | collective-permute-start | bytes 776 | tf_op jit(solution)/shard_map/ppermute | solution.py:30
  533.2 7.7 %collective-permute-start.15 = (f32[1,2,32]{2,1,0:T(2,128)S(1)}, f32[1,2,32]{2,1,0:T(2,128)S(1)}, u32[]{:S(2)}, u32[]{:S(2)}) collective-permute-start(f32[1,2,32]{2,1,0:T(2,128)S(1)} %bitcast.633), channel_id=1, source_target_pairs={{1,0},{2,1},{3,2},{4,3},{5,4},{6,5},{7,6},{0,7},{9,8},{10,9},{11,1... | collective-permute-start | bytes 776 | tf_op jit(solution)/shard_map/ppermute | solution.py:32
  536.3 5.3 collective-permute-start.13
  (14 other events, 181.2 us)
where the time goes:
time: 552 us; the launch traced here: 543 us
  local copies, waits for them, and re-layouts  158 us (29%)
  matrix products  130 us (24%)
  blocking collectives  82.9 us (15%)
  starting transfers between devices  80.5 us (15%)
  waiting for transfers between devices  56 us (10%)
  other arithmetic  33.3 us (6%)
    dot_general x84, matrix products, contract(): jnp.einsum(form, left, right, precision=lax.Precision.HIGHEST, preferred_...  130 us
    all_to_all x4, blocking collectives, relay_spectrum(): lax.all_to_all(values_in, 'gx', split_axis=4, concat_axis=4, tiled=True)  63.6 us
    unnamed x56, local copies, waits for them, and re-layouts  55.4 us
    another operation x9, local copies, waits for them, and re-layouts, correction(): jnp.stack([real_y, imag_y])  37.9 us
    all_to_all x4, waiting for transfers between devices, relay_spectrum(): lax.all_to_all(lax.all_to_all(values_in, 'gx', split_axis=4, concat_axis=...  27.4 us
    ppermute x8, starting transfers between devices, padded(): lax.ppermute(tail, axis, [(i, (i + 1) % count) for i in range(count)])  20.9 us
    all_to_all x2, blocking collectives, relay_spectrum(): lax.all_to_all(lax.all_to_all(values_in, 'gx', split_axis=4, concat_axis=...  19.3 us
    ppermute x8, starting transfers between devices, padded(): lax.ppermute(head, axis, [((i + 1) % count, i) for i in range(count)])  17.3 us
  transfers between devices with their start and end apart: 24, of which 17 were waited for; matrix products, arithmetic and copies ran while one was open for 2% of the time, Pallas kernels for 0%

commit v1 on v0

v1 whole, which is shorter than its diff:
```python
import math

import jax
import jax.numpy as jnp
import ml_dtypes
import numpy as np
from jax import lax
from jax.experimental import pallas as pl
from jax.experimental.pallas import tpu as pltpu
from jax.sharding import PartitionSpec as P

MESH = pl.DeviceIdType.MESH
F32 = jnp.float32
BF16 = jnp.bfloat16

ITERS = 3
SECTIONS = 2
GX, GY = 32, 8
DEVICES = GX * GY
POINTS = 1024
ROWS, COLS = POINTS // GX, POINTS // GY
STATIC = 10

lame_silicon = 1.2
lame_germanium = 0.9
shear_silicon = 1.0
shear_germanium = 0.8
lame_medium = 1.05
shear_medium = 0.9
elastic_weight = 2.0
bond_energy = 0.7
base_rate = 1.0


def split(values):
    high = values.astype(ml_dtypes.bfloat16)
    return high, (values - high.astype(np.float64)).astype(ml_dtypes.bfloat16)


def tables():
    index = np.arange(256)
    angle = 2 * np.pi * (np.outer(index, index) % 256) / 256
    dft_high, dft_low = split(np.concatenate([np.cos(angle), np.sin(angle)], 1))
    lane = np.arange(128)
    angle = 2 * np.pi * np.outer(index, lane % 4) / POINTS
    turn_x = np.stack([np.cos(angle), np.sin(angle)]).astype(np.float32)
    angle = 2 * np.pi * np.outer(np.arange(64) // 16, index) / POINTS
    turn_y = np.stack([np.cos(angle), np.sin(angle)]).astype(np.float32)
    part, freq, comp, quad = lane // 64, lane // 16 % 4, lane // 4 % 4, lane % 4
    turns = np.outer(quad, quad) % 4
    cos4, sin4 = np.array([1, 0, -1, 0])[turns], np.array([0, 1, 0, -1])[turns]
    same_freq = freq[:, None] == freq[None, :]
    same_part = part[:, None] == part[None, :]
    to_real = part[None, :] == 0
    used = (comp[None, :] < 3) & same_freq
    forward = np.where(same_part, cos4, np.where(to_real, sin4, -sin4))
    forward4 = np.concatenate([forward * (used & (comp[:, None] == c)) for c in range(3)], 1)
    inverse = np.where(same_part, cos4, np.where(to_real, -sin4, sin4))
    inverse = inverse * (used & (comp[:, None] == comp[None, :]))
    turned = np.concatenate([-inverse[:, 64:], inverse[:, :64]], 1)
    inverse4 = np.concatenate([inverse, turned], 1)
    return (
        dft_high,
        dft_low,
        turn_x,
        turn_y,
        np.concatenate([forward4, forward4], 0).astype(ml_dtypes.bfloat16),
        np.concatenate([inverse4, inverse4], 0).astype(ml_dtypes.bfloat16),
    )


def halves(values):
    high = values.astype(BF16)
    return high, (values - high.astype(F32)).astype(BF16)


def dot(left, right, dims):
    return lax.dot_general(left, right, (dims, ((), ())), preferred_element_type=F32)


def table_left(dft, values, dims):
    high, low = halves(values)
    return dot(dft[0][...], high, dims) + dot(dft[0][...], low, dims) + dot(dft[1][...], high, dims)


def table_right(dft, values, dims):
    high, low = halves(values)
    return dot(high, dft[0][...], dims) + dot(low, dft[0][...], dims) + dot(high, dft[1][...], dims)


def green_tables(device, green):
    shape = (256, 128)
    lane = lax.broadcasted_iota(jnp.int32, shape, 1)
    comp = lax.rem(lane // 4, 4)
    index_x = lax.broadcasted_iota(jnp.int32, shape, 0) + 256 * lax.rem(lane, 4)
    index_y = 4 * device + lax.rem(lane // 16, 4)
    unit = 2.0 * math.pi / POINTS
    a = jnp.where(index_x < POINTS // 2, index_x, index_x - POINTS).astype(F32) * unit
    b = jnp.where(index_y < POINTS // 2, index_y, index_y - POINTS).astype(F32) * unit
    ratio = (lame_medium + shear_medium) / (lame_medium + 2.0 * shear_medium)
    squared = a * a + b * b
    positive = squared > 0
    inverse_sq = jnp.where(positive, 1.0 / jnp.where(positive, squared, 1.0), 0.0)
    base = inverse_sq * (-1.0 / (shear_medium * POINTS * POINTS))
    edge_x = (index_x == POINTS // 2).astype(F32)
    edge_y = (index_y == POINTS // 2).astype(F32)
    odd = base * (1.0 - jnp.abs(edge_x - edge_y))
    aa, bb, ab = a * a, b * b, a * b
    xx_xx = (aa - ratio * aa * aa * inverse_sq) * base
    yy_yy = (bb - ratio * bb * bb * inverse_sq) * base
    xx_yy = -ratio * aa * bb * inverse_sq * base
    xx_xy = (ab - 2.0 * ratio * aa * ab * inverse_sq) * odd
    yy_xy = (ab - 2.0 * ratio * bb * ab * inverse_sq) * odd
    xy_xy = 0.5 * (aa + bb - 4.0 * ratio * aa * bb * inverse_sq) * base

    def pick(first, second, third):
        return jnp.where(
            comp == 0, first, jnp.where(comp == 1, second, jnp.where(comp == 2, third, 0.0))
        )

    green[0] = pick(xx_xx, xx_yy, 0.5 * xx_xy)
    green[1] = pick(xx_yy, yy_yy, 0.5 * yy_xy)
    green[2] = pick(xx_xy, yy_xy, xy_xy)


def spectral(received, dft, turn_x, forward4, inverse4, green):
    sign = jnp.where(lax.broadcasted_iota(jnp.int32, (256, 128), 1) < 64, 1.0, -1.0)
    swapped = pltpu.roll(received, 64, 1) * sign
    both = jnp.concatenate(
        [
            jnp.concatenate([received, swapped], 1),
            jnp.concatenate([swapped, -received], 1),
        ],
        0,
    )
    first = table_left(dft, both, ((1,), (0,)))
    turned = turn_x[0] * first[:, :128] + turn_x[1] * first[:, 128:]
    spread = dot(jnp.concatenate(halves(turned), 1), forward4[...], ((1,), (0,)))
    mapped = (
        green[0] * spread[:, :128] + green[1] * spread[:, 128:256] + green[2] * spread[:, 256:]
    )
    back = dot(jnp.concatenate(halves(mapped), 1), inverse4[...], ((1,), (0,)))
    plain, crossed = back[:, :128], back[:, 128:]
    values = turn_x[0] * plain + turn_x[1] * crossed
    crossed = turn_x[0] * crossed - turn_x[1] * plain
    return table_left(dft, jnp.concatenate([values, crossed], 0), ((1,), (0,)))


def four(parts, sign):
    (r0, r1, r2, r3), (i0, i1, i2, i3) = parts
    er, ei, dr, di = r0 + r2, i0 + i2, r0 - r2, i0 - i2
    fr, fi, gr, gi = r1 + r3, i1 + i3, r1 - r3, i1 - i3
    up_r, up_i = dr - gi, di + gr
    down_r, down_i = dr + gi, di - gr
    if sign < 0:
        up_r, up_i, down_r, down_i = down_r, down_i, up_r, up_i
    return (er + fr, up_r, er - fr, down_r), (ei + fi, up_i, ei - fi, down_i)


def forward_y(stress, dft, turn_y):
    parts = [[field[:, 256 * a : 256 * a + 256] for a in range(4)] for field in stress]
    real, imag = (jnp.concatenate(list(part), 0) for part in four(parts, -1))
    turned_real = turn_y[0] * real + turn_y[1] * imag
    turned_imag = turn_y[0] * imag - turn_y[1] * real
    rows = jnp.concatenate(
        [
            jnp.concatenate([turned_real, turned_imag], 1),
            jnp.concatenate([turned_imag, -turned_real], 1),
        ],
        0,
    )
    return table_left(dft, rows, ((1,), (1,)))


def inverse_y(received, dft, turn_y):
    across = received.T
    real, imag = across[:64], across[64:]
    rows = jnp.concatenate(
        [jnp.concatenate([real, -imag], 1), jnp.concatenate([imag, real], 1)], 0
    )
    both = table_right(dft, rows, ((1,), (1,)))
    real, imag = both[:64], both[64:]
    turned_real = turn_y[0] * real - turn_y[1] * imag
    turned_imag = turn_y[0] * imag + turn_y[1] * real
    parts = [
        [part[16 * j : 16 * j + 16] for j in range(4)] for part in (turned_real, turned_imag)
    ]
    return [jnp.concatenate(list(part), 1) for part in four(parts, 1)]


def local_stress(normal, shear, fraction):
    lame_field = lame_silicon + (lame_germanium - lame_silicon) * fraction
    shear_field = 2.0 * (shear_silicon + (shear_germanium - shear_silicon) * fraction)
    excess = normal - fraction
    trace = excess + pltpu.roll(excess, 4, 0)
    return lame_field * trace + shear_field * excess, shear_field * shear, excess


def ring(steps, size):
    return min(steps % size, -steps % size)


def kernel(
    occupancy,
    colour,
    direction,
    barrier,
    dft_high,
    dft_low,
    turn_x,
    turn_y,
    forward4,
    inverse4,
    strain_out,
    composition_out,
    green,
    normal,
    shear,
    fraction_pencil,
    packed,
    landed,
    fraction_sent,
    fraction_got,
    static,
    static_y,
    static_x,
    static_corner,
    strain_sent,
    strain_got,
    energy_sent,
    energy_got,
    gather_sem,
    send_sem,
    recv_sem,
    fraction_send,
    fraction_recv,
    static_send,
    static_recv,
    last_send,
    last_recv,
    edge_send,
    edge_recv,
):
    gx, gy = lax.axis_index("gx"), lax.axis_index("gy")
    me = gx * GY + gy
    dft = (dft_high, dft_low)
    z, core = lax.rem(gx // 2, 8), lax.rem(gx, 2)
    x, y = gy // 2, lax.rem(gy, 2) * 2 + gx // 16

    places = sorted(
        [(dx, dy, dc) for dx in range(4) for dy in range(4) for dc in range(2)],
        key=lambda t: -(ring(t[0], 4) + ring(t[1], 4) + 0.5 * t[2]),
    )
    bases = []
    for dx, dy, dc in places:
        x_there, y_there, c_there = lax.rem(x + dx, 4), lax.rem(y + dy, 4), lax.rem(core + dc, 2)
        bases.append((lax.rem(y_there, 2) * 16 + c_there, x_there * 2 + y_there // 2))

    def to_others(send):
        def step(i, carry):
            steps = jnp.where(lax.rem(i, 2) == 0, 4 + i // 2, 4 - (i + 1) // 2)
            z_there = lax.rem(z + steps, 8)
            for base_x, base_y in bases:
                send(base_x + 2 * z_there, base_y)
            return carry

        lax.fori_loop(0, 7, step, 0)
        for base_x, base_y in bases[:-1]:
            send(base_x + 2 * z, base_y)

    def row_of(device):
        return lax.rem(device, GY)

    entry = pltpu.get_barrier_semaphore()
    for i in range(1, GY):
        pl.semaphore_signal(entry, inc=1, device_id=(gx, row_of(gy + i)), device_id_type=MESH)

    def along_gx(sem):
        def step(i, carry):
            there = lax.rem(gx + i, GX)
            pl.semaphore_signal(sem, inc=1, device_id=(there, gy), device_id_type=MESH)
            return carry

        lax.fori_loop(1, GX, step, 0)

    along_gx(entry)

    for layer in range(2):
        static[layer] = occupancy[layer].astype(F32)
        static[2 + layer] = barrier[layer]
        static[4 + layer] = colour[layer].astype(F32)
        for section in range(SECTIONS):
            static[6 + 2 * section + layer] = direction[section, layer].astype(F32)
    for there in range(GY):
        rows = slice(4 * there, 4 * there + 4)
        fraction_sent[there] = jnp.concatenate([static[0, rows], static[1, rows]], 0)
    normal[...] = jnp.zeros_like(normal)
    shear[...] = jnp.zeros_like(shear)

    pl.semaphore_wait(entry, GX - 1 + GY - 1)
    along_gx(gather_sem)

    def gy_copy(i, source, target, send, recv):
        there = row_of(gy + i)
        return pltpu.make_async_remote_copy(
            source.at[there], target.at[gy], send, recv, device_id=(gx, there), device_id_type=MESH
        )

    for i in range(1, GY):
        gy_copy(i, fraction_sent, fraction_got, fraction_send, fraction_recv).start()
    fraction_got[gy] = fraction_sent[gy]
    green_tables(me, green)

    def wait_rows(source, target, send, recv, rows):
        copy = pltpu.make_async_remote_copy(
            source.at[pl.ds(0, rows)],
            target.at[pl.ds(0, rows)],
            send,
            recv,
            device_id=(gx + 1 - 2 * core, gy),
            device_id_type=MESH,
        )
        copy.wait_send()
        copy.wait_recv()

    wait_rows(fraction_sent, fraction_got, fraction_send, fraction_recv, GY - 1)
    upper = lax.broadcasted_iota(jnp.int32, (8, POINTS), 0) < 4
    pencil = jnp.concatenate([fraction_got[g] for g in range(GY)], 1)
    other = pltpu.roll(pencil, 4, 0)
    fraction_pencil[0] = jnp.where(upper, pencil, other)
    fraction_pencil[1] = jnp.where(upper, other, pencil)
    pl.semaphore_wait(gather_sem, GX - 1)

    def exchange(slot, rows):
        packed[slot, :, 0, :] = rows

        def send(there_x, there_y):
            pltpu.make_async_remote_copy(
                packed.at[slot, there_x * GY + there_y],
                landed.at[slot, me],
                send_sem.at[slot],
                recv_sem.at[slot],
                device_id=(there_x, there_y),
                device_id_type=MESH,
            ).start()

        to_others(send)
        landed[slot, me] = packed[slot, me]
        wait_rows(
            packed.at[slot], landed.at[slot], send_sem.at[slot], recv_sem.at[slot], DEVICES - 1
        )
        return landed[slot, :, 0, :]

    def sweep(i, carry):
        stress = []
        for p in range(2):
            stress_normal, stress_shear, _ = local_stress(normal[p], shear[p], fraction_pencil[p])
            stress.append(jnp.concatenate([stress_normal, stress_shear], 0))
        arrived = exchange(2 * i, forward_y(stress, dft, turn_y))
        arrived = exchange(
            2 * i + 1, spectral(arrived, dft, turn_x, forward4, inverse4, green)
        )
        change = inverse_y(arrived, dft, turn_y)
        for p in range(2):
            normal[p] += change[p][:8]
            shear[p] += change[p][8:]
        return carry

    up, down = lax.rem(gx + 1, GX), lax.rem(gx + GX - 1, GX)
    after, before = row_of(gy + 1), row_of(gy + GY - 1)
    first, last = pl.ds(0, 8), pl.ds(ROWS - 8, 8)
    halos = [
        (static, static_y.at[0], (gx, before)),
        (static, static_y.at[1], (gx, after)),
        (static.at[:, first], static_x.at[0], (down, gy)),
        (static.at[:, last], static_x.at[1], (up, gy)),
        (static.at[:, first], static_corner.at[0], (down, before)),
        (static.at[:, first], static_corner.at[1], (down, after)),
        (static.at[:, last], static_corner.at[2], (up, before)),
        (static.at[:, last], static_corner.at[3], (up, after)),
    ]
    halos = [
        pltpu.make_async_remote_copy(
            source, target, static_send.at[k], static_recv.at[k], device_id=there, device_id_type=MESH
        )
        for k, (source, target, there) in enumerate(halos)
    ]
    for copy in halos:
        copy.start()

    lax.fori_loop(0, ITERS, sweep, 0)

    energies = []
    for p in range(2):
        stress_normal, stress_shear, excess = local_stress(normal[p], shear[p], fraction_pencil[p])
        density = stress_normal * excess + 2.0 * stress_shear * shear[p]
        energies.append(0.5 * (density + pltpu.roll(density, 4, 0)))
    energy = jnp.where(upper, energies[0], energies[1])
    shears = jnp.where(upper, shear[0], pltpu.roll(shear[1], 4, 0))
    left = lax.broadcasted_iota(jnp.int32, (8, COLS), 1) < COLS // 2

    def block(values, g):
        return values[:, COLS * (g % GY) : COLS * (g % GY) + COLS]

    for g in range(GY):
        strain_sent[g, 0:8] = block(normal[0], g)
        strain_sent[g, 8:16] = block(normal[1], g)
        strain_sent[g, 16:24] = block(shears, g)
        energy_sent[g, :, :COLS] = block(energy, g)
        energy_sent[g, :, COLS:] = jnp.where(left, block(energy, g + 1), block(energy, g - 1))
    for i in range(1, GY):
        gy_copy(i, energy_sent, energy_got, last_send.at[0], last_recv.at[0]).start()
    for i in range(1, GY):
        gy_copy(i, strain_sent, strain_got, last_send.at[1], last_recv.at[1]).start()

    def edge_copy(g, slot, there):
        return pltpu.make_async_remote_copy(
            energy_sent.at[g],
            energy_got.at[GY + slot],
            edge_send.at[slot],
            edge_recv.at[slot],
            device_id=(there, g),
            device_id_type=MESH,
        )

    @pl.when(gy == 0)
    def _():
        for g in range(GY):
            edge_copy(g, 0, down).start()

    @pl.when(gy == GY - 1)
    def _():
        for g in range(GY):
            edge_copy(g, 1, up).start()

    energy_got[gy] = energy_sent[gy]
    strain_got[gy] = strain_sent[gy]

    for copy in halos:
        copy.wait()
    narrow = lax.broadcasted_iota(jnp.int32, (8, COLS), 0) < 4
    left_block = lax.broadcasted_iota(jnp.int32, (ROWS, COLS), 1) < COLS // 2

    def extended(k):
        side = jnp.where(left_block, static_y[0, k], static_y[1, k])
        edge = jnp.where(narrow, static_x[0, k], static_x[1, k])
        after_edge = jnp.where(narrow, static_corner[0, k], static_corner[2, k])
        before_edge = jnp.where(narrow, static_corner[1, k], static_corner[3, k])
        corner = jnp.where(left, after_edge, before_edge)
        return jnp.concatenate(
            [
                jnp.concatenate([static[k], side], 1),
                jnp.concatenate([edge, corner], 1),
            ],
            0,
        )

    fields = [extended(k) for k in range(STATIC)]

    wait_rows(energy_sent, energy_got, last_send.at[0], last_recv.at[0], GY - 1)
    for slot in range(2):
        edge_copy(0, slot, up).wait_recv()
    low = lax.broadcasted_iota(jnp.int32, (8, 2 * COLS), 0) < 4

    for layer in range(2):
        pieces = []
        for pair in range(GY // 2 + 1):
            one, two = energy_got[2 * pair], energy_got[2 * pair + 1]
            if layer == 0:
                pieces.append(jnp.where(low, one, pltpu.roll(two, 4, 0)))
            else:
                pieces.append(jnp.where(low, pltpu.roll(one, 4, 0), two))
        drive = fields[2 + layer] + elastic_weight * jnp.concatenate(pieces, 0) + base_rate
        sites = fields[layer]
        tall, wide = ROWS + 8, 2 * COLS
        for section in range(SECTIONS):
            way = fields[6 + 2 * section + layer]
            above, below = pltpu.roll(sites, 1, 0), pltpu.roll(sites, tall - 1, 0)
            ahead, behind = pltpu.roll(sites, wide - 1, 1), pltpu.roll(sites, 1, 1)
            neighbours = above + below + behind + ahead
            rate = 1.0 / (1.0 + jnp.exp(bond_energy * neighbours - drive))
            target = jnp.where(
                way == 0.0,
                below,
                jnp.where(way == 1.0, above, jnp.where(way == 2.0, ahead, behind)),
            )
            flux = jnp.where(
                fields[4 + layer] == float(section), rate * sites * (1.0 - target), 0.0
            )
            parted = [jnp.where(way == float(number), flux, 0.0) for number in range(4)]
            sites = (
                sites
                - flux
                + (
                    pltpu.roll(parted[0], 1, 0)
                    + pltpu.roll(parted[1], tall - 1, 0)
                    + pltpu.roll(parted[2], 1, 1)
                    + pltpu.roll(parted[3], wide - 1, 1)
                )
            )
        composition_out[layer] = sites[:ROWS, :COLS]

    wait_rows(strain_sent, strain_got, last_send.at[1], last_recv.at[1], GY - 1)
    for g in range(GY):
        rows = slice(4 * g, 4 * g + 4)
        for layer in range(2):
            strain_out[0, layer, rows] = strain_got[g, 8 * layer : 8 * layer + 4]
            strain_out[1, layer, rows] = strain_got[g, 8 * layer + 4 : 8 * layer + 8]
            strain_out[2, layer, rows] = strain_got[g, 16 + 4 * layer : 20 + 4 * layer]

    @pl.when(gy == 0)
    def _():
        for g in range(GY):
            edge_copy(g, 0, down).wait_send()

    @pl.when(gy == GY - 1)
    def _():
        for g in range(GY):
            edge_copy(g, 1, up).wait_send()


def on_device(occupancy, colour, hop_direction, barrier):
    operands = (occupancy, colour, hop_direction, barrier) + tuple(
        jnp.asarray(table) for table in tables()
    )
    vmem = pl.BlockSpec(memory_space=pltpu.VMEM)
    dma = pltpu.SemaphoreType.DMA
    return pl.pallas_call(
        kernel,
        out_shape=(
            jax.ShapeDtypeStruct((3, 2, ROWS, COLS), F32),
            jax.ShapeDtypeStruct((2, ROWS, COLS), F32),
        ),
        in_specs=[vmem] * len(operands),
        out_specs=(vmem, vmem),
        scratch_shapes=[
            pltpu.VMEM((3, 256, 128), F32),
            pltpu.VMEM((2, 8, POINTS), F32),
            pltpu.VMEM((2, 8, POINTS), F32),
            pltpu.VMEM((2, 8, POINTS), F32),
            pltpu.VMEM((2 * ITERS, DEVICES, 1, 128), F32),
            pltpu.VMEM((2 * ITERS, DEVICES, 1, 128), F32),
            pltpu.VMEM((GY, 8, COLS), F32),
            pltpu.VMEM((GY, 8, COLS), F32),
            pltpu.VMEM((STATIC, ROWS, COLS), F32),
            pltpu.VMEM((2, STATIC, ROWS, COLS), F32),
            pltpu.VMEM((2, STATIC, 8, COLS), F32),
            pltpu.VMEM((4, STATIC, 8, COLS), F32),
            pltpu.VMEM((GY, 24, COLS), F32),
            pltpu.VMEM((GY, 24, COLS), F32),
            pltpu.VMEM((GY, 8, 2 * COLS), F32),
            pltpu.VMEM((GY + 2, 8, 2 * COLS), F32),
            pltpu.SemaphoreType.REGULAR,
            dma((2 * ITERS,)),
            dma((2 * ITERS,)),
            dma,
            dma,
            dma((8,)),
            dma((8,)),
            dma((2,)),
            dma((2,)),
            dma((2,)),
            dma((2,)),
        ],
        compiler_params=pltpu.CompilerParams(
            collective_id=0, has_side_effects=True, vmem_limit_bytes=40 * 1024 * 1024
        ),
        name="film",
    )(*operands)


def solution(mesh):
    placed = (
        P(None, "gx", "gy"),
        P(None, "gx", "gy"),
        P(None, None, "gx", "gy"),
        P(None, "gx", "gy"),
    )
    return jax.shard_map(
        on_device,
        mesh=mesh,
        in_specs=placed,
        out_specs=(P(None, None, "gx", "gy"), P(None, "gx", "gy")),
        check_vma=False,
    )
```

time: 552 us -> 92.6 us (0.17); the launches traced: 543 us -> 92.1 us
  local copies, waits for them, and re-layouts: 158 us -> 9.95 us
  matrix products: 130 us -> 0 us
  blocking collectives: 82.9 us -> 0 us
  Pallas kernels: 0 us -> 81.5 us
  starting transfers between devices: 80.5 us -> 0 us
  waiting for transfers between devices: 56 us -> 0 us
  other arithmetic: 33.3 us -> 0 us
    dot_general x84 -> x0, matrix products: 130 us -> none  [contract(): jnp.einsum(form, left, right, precision=lax.Precision.HIGHEST, preferred_...]
    all_to_all x6 -> x0, blocking collectives: 82.9 us -> none  [the longest x4 63.6 us: relay_spectrum(): lax.all_to_all(values_in, 'gx', split_axis=4, concat_axis=4, tiled=True)]
    pallas_call x0 -> x1, Pallas kernels: none -> 81.5 us  [on_device(): pl.pallas_call(kernel, out_shape=(jax.ShapeDtypeStruct((3, 2, ROWS, COLS)...]
    all_to_all x8 -> x0, waiting for transfers between devices: 50.7 us -> none  [the longest x4 27.4 us: relay_spectrum(): lax.all_to_all(lax.all_to_all(values_in, 'gx', split_axis=4, concat_axis=...]
    another operation x25 -> x0, local copies, waits for them, and re-layouts: 48 us -> none  [the longest x9 37.9 us: correction(): jnp.stack([real_y, imag_y])]
    unnamed x56 -> x22, local copies, waits for them, and re-layouts: 55.4 us -> 9.95 us
    all_to_all x8 -> x0, starting transfers between devices: 42.2 us -> none  [the longest x2 17.2 us: relay_spectrum(): lax.all_to_all(values_in, 'gx', split_axis=4, concat_axis=4, tiled=True)]
    ppermute x16 -> x0, starting transfers between devices: 38.3 us -> none  [the longest x8 20.9 us: padded(): lax.ppermute(tail, axis, [(i, (i + 1) % count) for i in range(count)])]
  transfers between devices with their start and end apart: 24 -> 0, of which waited for: 17 -> 0; matrix products, arithmetic and copies ran while one was open for 2% -> 0% of each run, Pallas kernels for 0% -> 0%
where the time goes in v1:
time: 92.6 us; the launch traced here: 92.1 us
  Pallas kernels  81.5 us (88%)
  local copies, waits for them, and re-layouts  9.95 us (11%)
    pallas_call x1, Pallas kernels, on_device(): pl.pallas_call(kernel, out_shape=(jax.ShapeDtypeStruct((3, 2, ROWS, COLS)...  81.5 us
    unnamed x22, local copies, waits for them, and re-layouts  9.95 us

profile of v1, /device:TPU:1, one launch (start us, length us, event | category | flops | bytes accessed | tf_op | source)
XLA Modules:
  0.0 92.1 jit_solution(14976639306488314184)
XLA Ops:
  0.6 0.0 copy-start
  0.6 0.9 %copy-done = f32[2,256,128]{2,1,0:T(8,128)S(1)} copy-done((f32[2,256,128]{2,1,0:T(8,128)S(1)}, f32[2,256,128]{2,1,0:T(8,128)}, u32[]{:S(2)}) %copy-start) | copy-done | bytes 262168
  1.6 0.0 copy-start.1
  1.6 0.9 %copy-done.1 = bf16[256,512]{1,0:T(8,128)(2,1)S(1)} copy-done((bf16[256,512]{1,0:T(8,128)(2,1)S(1)}, bf16[256,512]{1,0:T(8,128)(2,1)}, u32[]{:S(2)}) %copy-start.1) | copy-done | bytes 262168
  2.5 0.0 copy-start.2
  2.5 0.9 %copy-done.2 = bf16[256,512]{1,0:T(8,128)(2,1)S(1)} copy-done((bf16[256,512]{1,0:T(8,128)(2,1)S(1)}, bf16[256,512]{1,0:T(8,128)(2,1)}, u32[]{:S(2)}) %copy-start.2) | copy-done | bytes 262168
  3.5 0.0 copy-start.3
  3.5 0.9 %copy-done.3 = bf16[256,384]{1,0:T(8,128)(2,1)S(1)} copy-done((bf16[256,384]{1,0:T(8,128)(2,1)S(1)}, bf16[256,384]{1,0:T(8,128)(2,1)}, u32[]{:S(2)}) %copy-start.3) | copy-done | bytes 196632
  4.4 0.0 copy-start.4
  4.4 0.9 copy-done.4
  5.3 0.0 copy-start.5
  5.3 0.9 copy-done.5
  6.2 0.0 copy-start.6
  6.2 0.8 copy-done.6
  7.1 0.0 copy-start.7
  7.1 0.8 copy-done.7
  7.8 0.0 copy-start.8
  7.8 0.8 copy-done.8
  8.6 0.0 copy-start.9
  8.6 0.8 copy-done.9
  9.3 81.5 %film.1 = (f32[3,2,32,128]{3,2,1,0:T(8,128)S(1)}, f32[2,32,128]{2,1,0:T(8,128)S(1)}) custom-call(s32[2,32,128]{2,1,0:T(8,128)S(1)} %copy-done.7, s32[2,32,128]{2,1,0:T(8,128)S(1)} %copy-done.8, s32[2,2,32,128]{3,2,1,0:T(8,128)S(1)} %copy-done.6, f32[2,32,128]{2,1,0:T(8,128)S(1)} %copy-done.9, bf16[256,512]{1,0:T(8,128)(2,1)S(1)} %copy-done.2, ...), custom_call_target="tpu_custom_call" | custom-call | tf_op jit(solution)/shard_map/film/pallas_call | solution.py:528
  90.9 0.6 copy.14
  91.5 0.6 copy.15
Async XLA Ops:
  0.6 1.0 %copy-start = (f32[2,256,128]{2,1,0:T(8,128)S(1)}, f32[2,256,128]{2,1,0:T(8,128)}, u32[]{:S(2)}) copy-start(f32[2,256,128]{2,1,0:T(8,128)} %constant.14.clone.turn_x) | copy-start | bytes 786436
  1.6 0.9 %copy-start.1 = (bf16[256,512]{1,0:T(8,128)(2,1)S(1)}, bf16[256,512]{1,0:T(8,128)(2,1)}, u32[]{:S(2)}) copy-start(bf16[256,512]{1,0:T(8,128)(2,1)} %constant.13.clone.dft_low) | copy-start | bytes 786436
  2.5 0.9 %copy-start.2 = (bf16[256,512]{1,0:T(8,128)(2,1)S(1)}, bf16[256,512]{1,0:T(8,128)(2,1)}, u32[]{:S(2)}) copy-start(bf16[256,512]{1,0:T(8,128)(2,1)} %constant.12.clone.dft_high) | copy-start | bytes 786436
  3.5 0.9 %copy-start.3 = (bf16[256,384]{1,0:T(8,128)(2,1)S(1)}, bf16[256,384]{1,0:T(8,128)(2,1)}, u32[]{:S(2)}) copy-start(bf16[256,384]{1,0:T(8,128)(2,1)} %constant.16.clone.forward4) | copy-start | bytes 589828
  4.4 0.9 copy-start.4
  5.3 0.9 copy-start.5
  6.2 0.8 copy-start.6
  7.1 0.8 copy-start.7
  7.8 0.8 copy-start.8
  8.6 0.8 copy-start.9

commit v2 on v1

v2 whole, which is shorter than its diff:
```python
import math

import jax
import jax.numpy as jnp
import ml_dtypes
import numpy as np
from jax import lax
from jax.experimental import pallas as pl
from jax.experimental.pallas import tpu as pltpu
from jax.sharding import PartitionSpec as P

MESH = pl.DeviceIdType.MESH
F32 = jnp.float32
BF16 = jnp.bfloat16

ITERS = 3
SECTIONS = 2
GX, GY = 32, 8
DEVICES = GX * GY
POINTS = 1024
ROWS, COLS = POINTS // GX, POINTS // GY
STATIC = 10

lame_silicon = 1.2
lame_germanium = 0.9
shear_silicon = 1.0
shear_germanium = 0.8
lame_medium = 1.05
shear_medium = 0.9
elastic_weight = 2.0
bond_energy = 0.7
base_rate = 1.0


def split(values):
    high = values.astype(ml_dtypes.bfloat16)
    return high, (values - high.astype(np.float64)).astype(ml_dtypes.bfloat16)


def waves(angle, axis):
    return np.concatenate([np.cos(angle), np.sin(angle)], axis)


def tables():
    index = np.arange(256)
    angle = 2 * np.pi * (np.outer(index, index) % 256) / 256
    coarse = 2 * np.pi * (np.outer(index, index // 8) % 32) / 32
    dft = split(waves(angle, 1)) + split(waves(coarse, 1))
    lane = np.arange(128)
    turn_x = waves(2 * np.pi * np.outer(index, lane % 4) / POINTS, 0)
    turn_first = waves(2 * np.pi * np.outer(index, lane // 16 * 4 + lane % 4) / POINTS, 0)
    turn_y = waves(2 * np.pi * np.outer(np.arange(64) // 16, index) / POINTS, 0).reshape(2, 64, 256)
    stress = -2.0 * (lame_germanium + shear_germanium)
    angle = 2 * np.pi * np.outer(np.arange(16) // 4, np.arange(POINTS)) / POINTS
    turn_own = stress * np.stack([np.cos(angle), np.sin(angle)])
    turn_own = turn_own.reshape(2, 16, GY, COLS).transpose(2, 0, 1, 3)
    part, freq, comp, quad = lane // 64, lane // 16 % 4, lane // 4 % 4, lane % 4
    turns = np.outer(quad, quad) % 4
    cos4, sin4 = np.array([1, 0, -1, 0])[turns], np.array([0, 1, 0, -1])[turns]
    same_freq = freq[:, None] == freq[None, :]
    same_part = part[:, None] == part[None, :]
    to_real = part[None, :] == 0
    used = (comp[None, :] < 3) & same_freq
    forward = np.where(same_part, cos4, np.where(to_real, sin4, -sin4))
    forward4 = np.concatenate([forward * (used & (comp[:, None] == c)) for c in range(3)], 1)
    inverse = np.where(same_part, cos4, np.where(to_real, -sin4, sin4))
    inverse = inverse * (used & (comp[:, None] == comp[None, :]))
    turned = np.concatenate([-inverse[:, 64:], inverse[:, :64]], 1)
    inverse4 = np.concatenate([inverse, turned], 1)
    first4 = np.where((comp == 0)[:, None], forward4[:, :128], 0)
    picked = np.zeros((256, 128))
    for p in range(2):
        for n in range(128):
            picked[p * 128 + n] = first4[p * 64 + n // 4 % 4 * 16 + n % 4]
    small = np.concatenate([forward4, inverse4, picked[:128], picked[128:]], 1)
    return (
        np.concatenate(dft, 0),
        small.astype(ml_dtypes.bfloat16),
        np.concatenate([turn_x, turn_first], 0).reshape(4, 256, 128).astype(np.float32),
        turn_y.astype(np.float32),
        turn_own.astype(np.float32),
    )


def halves(values):
    high = values.astype(BF16)
    return high, (values - high.astype(F32)).astype(BF16)


def dot(left, right, dims):
    return lax.dot_general(left, right, (dims, ((), ())), preferred_element_type=F32)


def table_left(dft, values):
    high, low = halves(values)
    wide = dot(dft[0][...], jnp.concatenate([high, low], 1), ((1,), (0,)))
    return wide[:, :128] + wide[:, 128:] + dot(dft[1][...], high, ((1,), (0,)))


def table_left_turned(dft, rows):
    high, low = halves(rows)
    wide = dot(dft[0][...], jnp.concatenate([high, low], 0), ((1,), (1,)))
    return wide[:, :128] + wide[:, 128:] + dot(dft[1][...], high, ((1,), (1,)))


def three(left, right, dims):
    return dot(left[0], right[0], dims) + dot(left[0], right[1], dims) + dot(left[1], right[0], dims)


def exact(values, table):
    return dot(jnp.concatenate(halves(values), 1), jnp.concatenate([table, table], 0), ((1,), (0,)))


def green_tables(device, green):
    shape = (256, 128)
    lane = lax.broadcasted_iota(jnp.int32, shape, 1)
    comp = lax.rem(lane // 4, 4)
    index_x = lax.broadcasted_iota(jnp.int32, shape, 0) + 256 * lax.rem(lane, 4)
    index_y = 4 * device + lax.rem(lane // 16, 4)
    unit = 2.0 * math.pi / POINTS
    a = jnp.where(index_x < POINTS // 2, index_x, index_x - POINTS).astype(F32) * unit
    b = jnp.where(index_y < POINTS // 2, index_y, index_y - POINTS).astype(F32) * unit
    ratio = (lame_medium + shear_medium) / (lame_medium + 2.0 * shear_medium)
    squared = a * a + b * b
    positive = squared > 0
    inverse_sq = jnp.where(positive, 1.0 / jnp.where(positive, squared, 1.0), 0.0)
    base = inverse_sq * (-1.0 / (shear_medium * POINTS * POINTS))
    edge_x = (index_x == POINTS // 2).astype(F32)
    edge_y = (index_y == POINTS // 2).astype(F32)
    odd = base * (1.0 - jnp.abs(edge_x - edge_y))
    aa, bb, ab = a * a, b * b, a * b
    xx_xx = (aa - ratio * aa * aa * inverse_sq) * base
    yy_yy = (bb - ratio * bb * bb * inverse_sq) * base
    xx_yy = -ratio * aa * bb * inverse_sq * base
    xx_xy = (ab - 2.0 * ratio * aa * ab * inverse_sq) * odd
    yy_xy = (ab - 2.0 * ratio * bb * ab * inverse_sq) * odd
    xy_xy = 0.5 * (aa + bb - 4.0 * ratio * aa * bb * inverse_sq) * base

    def pick(first, second, third):
        return jnp.where(
            comp == 0, first, jnp.where(comp == 1, second, jnp.where(comp == 2, third, 0.0))
        )

    green[0] = pick(xx_xx, xx_yy, 0.5 * xx_xy)
    green[1] = pick(xx_yy, yy_yy, 0.5 * yy_xy)
    green[2] = pick(xx_xy, yy_xy, xy_xy)


def crossing(shape):
    return jnp.where(lax.broadcasted_iota(jnp.int32, shape, 1) < 64, 1.0, -1.0)


def spectral(received, dft, turn, small, green):
    sign = crossing((256, 128))
    swapped = pltpu.roll(received, 64, 1) * sign
    first = table_left(dft, jnp.concatenate([received, swapped], 0))
    turned = turn[0] * first + turn[1] * (pltpu.roll(first, 64, 1) * sign)
    spread = exact(turned, small[:, :384])
    mapped = (
        green[0] * spread[:, :128] + green[1] * spread[:, 128:256] + green[2] * spread[:, 256:]
    )
    return spectral_back(mapped, dft, turn, small)


def spectral_back(mapped, dft, turn, small):
    back = exact(mapped, small[:, 384:640])
    plain, crossed = back[:, :128], back[:, 128:]
    values = turn[0] * plain + turn[1] * crossed
    crossed = turn[0] * crossed - turn[1] * plain
    return table_left(dft, jnp.concatenate([values, crossed], 0))


def spectral_first(received, dft, coarse, turn, small, green):
    real, imag = received[:, :128], received[:, 128:]
    both = jnp.concatenate(
        [jnp.concatenate([real, imag], 1), jnp.concatenate([imag, -real], 1)], 0
    )
    first = three([part[...] for part in coarse], halves(both), ((1,), (0,)))
    real, imag = first[:, :128], first[:, 128:]
    real, imag = turn[2] * real + turn[3] * imag, turn[2] * imag - turn[3] * real
    spread = exact(
        jnp.concatenate([real, imag], 1),
        jnp.concatenate([small[:, 640:768], small[:, 768:896]], 0),
    )
    return spectral_back((green[0] + green[1]) * spread, dft, turn, small)


def first_y(fields, dft, turn, odd):
    upper = lax.broadcasted_iota(jnp.int32, (8, COLS), 0) < 4
    spread = []
    for field in fields:
        pieces = []
        for t in range(ROWS // 8):
            tile = field[8 * t : 8 * t + 8]
            other = pltpu.roll(tile, 4, 0)
            one, two = jnp.where(upper, tile, other), jnp.where(upper, other, tile)
            pieces += [one, one, two, two]
        spread.append(jnp.concatenate(pieces, 0))
    real, imag = spread
    cos, sin = (jnp.concatenate([turn[k]] * 8, 0) for k in range(2))
    real, imag = cos * real + sin * imag, cos * imag - sin * real
    rows = jnp.concatenate(
        [jnp.concatenate([real, imag], 1), jnp.concatenate([imag, -real], 1)], 0
    )
    table = [jnp.concatenate([part[:, :128], part[:, 256:384]], 1) for part in dft]
    out = three(table, halves(rows), ((1,), (1,)))
    flip = lax.rem(lax.broadcasted_iota(jnp.int32, out.shape, 0), 2) * odd
    return out * (1 - 2 * flip).astype(F32)


def four(parts, sign):
    (r0, r1, r2, r3), (i0, i1, i2, i3) = parts
    er, ei, dr, di = r0 + r2, i0 + i2, r0 - r2, i0 - i2
    fr, fi, gr, gi = r1 + r3, i1 + i3, r1 - r3, i1 - i3
    up_r, up_i = dr - gi, di + gr
    down_r, down_i = dr + gi, di - gr
    if sign < 0:
        up_r, up_i, down_r, down_i = down_r, down_i, up_r, up_i
    return (er + fr, up_r, er - fr, down_r), (ei + fi, up_i, ei - fi, down_i)


def forward_y(stress, dft, turn_y):
    parts = [[field[:, 256 * a : 256 * a + 256] for a in range(4)] for field in stress]
    real, imag = (jnp.concatenate(list(part), 0) for part in four(parts, -1))
    turned_real = turn_y[0] * real + turn_y[1] * imag
    turned_imag = turn_y[0] * imag - turn_y[1] * real
    rows = jnp.concatenate(
        [
            jnp.concatenate([turned_real, turned_imag], 1),
            jnp.concatenate([turned_imag, -turned_real], 1),
        ],
        0,
    )
    return table_left_turned(dft, rows)


def inverse_y(received, dft, turn_y):
    across = received.T
    real, imag = across[:64], across[64:]
    rows = jnp.concatenate(
        [jnp.concatenate([real, -imag], 1), jnp.concatenate([imag, real], 1)], 0
    )
    both = three(halves(rows), [part[...] for part in dft], ((1,), (1,)))
    real, imag = both[:64], both[64:]
    turned_real = turn_y[0] * real - turn_y[1] * imag
    turned_imag = turn_y[0] * imag + turn_y[1] * real
    parts = [
        [part[16 * j : 16 * j + 16] for j in range(4)] for part in (turned_real, turned_imag)
    ]
    return [jnp.concatenate(list(part), 1) for part in four(parts, 1)]


def local_stress(normal, shear, fraction):
    lame_field = lame_silicon + (lame_germanium - lame_silicon) * fraction
    shear_field = 2.0 * (shear_silicon + (shear_germanium - shear_silicon) * fraction)
    excess = normal - fraction
    trace = excess + pltpu.roll(excess, 4, 0)
    return lame_field * trace + shear_field * excess, shear_field * shear, excess


def ring(steps, size):
    return min(steps % size, -steps % size)


def kernel(
    occupancy_in,
    colour_in,
    direction_in,
    barrier_in,
    dft_in,
    small_in,
    turn_in,
    turn_y_in,
    turn_own_in,
    strain_out,
    composition_out,
    occupancy,
    colour,
    direction,
    barrier,
    dfts,
    small,
    turn,
    turn_y,
    turn_own,
    green,
    normal,
    shear,
    fraction_pencil,
    first_sent,
    first_got,
    packed,
    landed,
    fraction_sent,
    fraction_got,
    static,
    rows_sent,
    rows_got,
    cols_sent,
    cols_got,
    corner_got,
    fields,
    strain_sent,
    strain_got,
    energy_sent,
    energy_got,
    input_sem,
    first_sem,
    send_sem,
    recv_sem,
    fraction_sem,
    halo_send,
    halo_recv,
    last_send,
    last_recv,
    edge_send,
    edge_recv,
):
    gx, gy = lax.axis_index("gx"), lax.axis_index("gy")
    me = gx * GY + gy
    z, core = lax.rem(gx // 2, 8), lax.rem(gx, 2)
    x, y = gy // 2, lax.rem(gy, 2) * 2 + gx // 16

    inputs = [
        (occupancy_in, occupancy),
        (dft_in, dfts),
        (turn_own_in.at[gy], turn_own),
        (barrier_in, barrier),
        (colour_in, colour),
        (direction_in, direction),
        (small_in, small),
        (turn_in, turn),
        (turn_y_in, turn_y),
    ]
    inputs = [
        pltpu.make_async_copy(source, target, input_sem.at[k])
        for k, (source, target) in enumerate(inputs)
    ]
    for copy in inputs:
        copy.start()

    places = sorted(
        [(dx, dy, dc) for dx in range(4) for dy in range(4) for dc in range(2)],
        key=lambda t: -(ring(t[0], 4) + ring(t[1], 4) + 0.5 * t[2]),
    )
    bases = []
    for dx, dy, dc in places:
        x_there, y_there, c_there = lax.rem(x + dx, 4), lax.rem(y + dy, 4), lax.rem(core + dc, 2)
        bases.append((lax.rem(y_there, 2) * 16 + c_there, x_there * 2 + y_there // 2))

    def to_others(send):
        def step(i, carry):
            steps = jnp.where(lax.rem(i, 2) == 0, 4 + i // 2, 4 - (i + 1) // 2)
            z_there = lax.rem(z + steps, 8)
            for base_x, base_y in bases:
                send(base_x + 2 * z_there, base_y)
            return carry

        lax.fori_loop(0, 7, step, 0)
        for base_x, base_y in bases[:-1]:
            send(base_x + 2 * z, base_y)

    entry = pltpu.get_barrier_semaphore()
    to_others(
        lambda there_x, there_y: pl.semaphore_signal(
            entry, inc=1, device_id=(there_x, there_y), device_id_type=MESH
        )
    )

    dft = (dfts.at[pl.ds(0, 256)], dfts.at[pl.ds(256, 256)])
    coarse = (dfts.at[pl.ds(512, 256)], dfts.at[pl.ds(768, 256)])

    for copy in inputs[:3]:
        copy.wait()
    for layer in range(2):
        static[layer] = occupancy[layer].astype(F32)
    rows = first_y([static[0], static[1]], dft, turn_own, lax.rem(gy, 2))
    first_sent[:, 0, :] = rows[:, :128]
    first_sent[:, 1, :] = rows[:, 128:]
    first_got[me] = first_sent[me]
    for there in range(GY):
        part = slice(4 * there, 4 * there + 4)
        fraction_sent[there] = jnp.concatenate([static[0, part], static[1, part]], 0)
    fraction_got[gy] = fraction_sent[gy]

    pl.semaphore_wait(entry, DEVICES - 1)

    def send_first(there_x, there_y):
        pltpu.make_async_remote_copy(
            first_sent.at[there_x * GY + there_y],
            first_got.at[me],
            first_sem.at[0],
            first_sem.at[1],
            device_id=(there_x, there_y),
            device_id_type=MESH,
        ).start()

    to_others(send_first)

    def total(source, target, send, recv, rows):
        return pltpu.make_async_remote_copy(
            source.at[pl.ds(0, rows)],
            target.at[pl.ds(0, rows)],
            send,
            recv,
            device_id=(gx + 1 - 2 * core, gy),
            device_id_type=MESH,
        )

    offsets = sorted(
        [(dx, dy) for dx in range(4) for dy in range(2) if dx + dy > 0],
        key=lambda t: -(ring(t[0], 4) + 2 * t[1]),
    )
    peers = [lax.rem(x + dx, 4) * 2 + lax.rem(gy + dy, 2) for dx, dy in offsets]

    def to_peers(source, target, send, recv):
        for there in peers:
            pltpu.make_async_remote_copy(
                source.at[there],
                target.at[gy],
                send,
                recv,
                device_id=(gx, there),
                device_id_type=MESH,
            ).start()
        return total(source, target, send, recv, GY - 1)

    fraction_copies = to_peers(fraction_sent, fraction_got, fraction_sem.at[0], fraction_sem.at[1])

    for copy in inputs[3:]:
        copy.wait()
    for layer in range(2):
        static[2 + layer] = barrier[layer]
        static[4 + layer] = colour[layer].astype(F32)
        for section in range(SECTIONS):
            static[6 + 2 * section + layer] = direction[section, layer].astype(F32)
    upper = lax.broadcasted_iota(jnp.int32, (8, COLS), 0) < 4
    for kind in range(STATIC // 2):
        one, two = static[2 * kind], static[2 * kind + 1]
        rows_sent[0, kind] = jnp.where(upper, one[:8], pltpu.roll(two[:8], 4, 0))
        rows_sent[1, kind] = jnp.where(upper, pltpu.roll(one[-8:], 4, 0), two[-8:])
    flat = [static[k] for k in range(STATIC)] + [jnp.zeros((64, COLS), F32)]
    across = jnp.concatenate(flat, 0).T
    cols_sent[0] = across[:8]
    cols_sent[1] = across[-8:]

    up, down = lax.rem(gx + 1, GX), lax.rem(gx + GX - 1, GX)
    after, before = lax.rem(gy + 1, GY), lax.rem(gy + GY - 1, GY)
    halos = [
        (rows_sent.at[0], rows_got.at[0], (down, gy)),
        (rows_sent.at[1], rows_got.at[1], (up, gy)),
        (cols_sent.at[0], cols_got.at[0], (gx, before)),
        (cols_sent.at[1], cols_got.at[1], (gx, after)),
        (cols_sent.at[0], corner_got.at[0], (down, before)),
        (cols_sent.at[1], corner_got.at[1], (down, after)),
        (cols_sent.at[0], corner_got.at[2], (up, before)),
        (cols_sent.at[1], corner_got.at[3], (up, after)),
    ]
    halos = [
        pltpu.make_async_remote_copy(
            source, target, halo_send.at[k], halo_recv.at[k], device_id=there, device_id_type=MESH
        )
        for k, (source, target, there) in enumerate(halos)
    ]
    for copy in halos:
        copy.start()
    green_tables(me, green)

    total(first_sent, first_got, first_sem.at[0], first_sem.at[1], DEVICES - 1).wait_recv()
    received = jnp.concatenate([first_got[:, 0, :], first_got[:, 1, :]], 1)

    def start_exchange(slot, rows):
        packed[slot, :, 0, :] = rows

        def send(there_x, there_y):
            pltpu.make_async_remote_copy(
                packed.at[slot, there_x * GY + there_y],
                landed.at[slot, me],
                send_sem.at[slot],
                recv_sem.at[slot],
                device_id=(there_x, there_y),
                device_id_type=MESH,
            ).start()

        to_others(send)
        landed[slot, me] = packed[slot, me]

    def exchanged(slot):
        return total(
            packed.at[slot], landed.at[slot], send_sem.at[slot], recv_sem.at[slot], DEVICES - 1
        )

    def end_exchange(slot):
        exchanged(slot).wait_recv()
        return landed[slot, :, 0, :]

    start_exchange(0, spectral_first(received, dft, coarse, turn, small, green))

    fraction_copies.wait_recv()
    pencil = jnp.concatenate([fraction_got[g] for g in range(GY)], 1)
    other = pltpu.roll(pencil, 4, 0)
    upper_wide = lax.broadcasted_iota(jnp.int32, (8, POINTS), 0) < 4
    fraction_pencil[0] = jnp.where(upper_wide, pencil, other)
    fraction_pencil[1] = jnp.where(upper_wide, other, pencil)
    for copy in halos:
        copy.wait_recv()

    def side(ahead, behind):
        gap = jnp.zeros((COLS - 16, 384), F32)
        return jnp.concatenate([ahead, gap, behind], 0).T

    beside = side(cols_got[0], cols_got[1])
    below = side(corner_got[0], corner_got[1])
    above = side(corner_got[2], corner_got[3])
    for k in range(STATIC):
        kind, layer = k // 2, k % 2
        part = slice(ROWS * k, ROWS * k + ROWS)
        fields[k, :ROWS, :COLS] = static[k]
        fields[k, :ROWS, COLS:] = beside[part]
        low, high = rows_got[0, kind], rows_got[1, kind]
        if layer == 0:
            high = pltpu.roll(high, 4, 0)
        else:
            low = pltpu.roll(low, 4, 0)
        fields[k, ROWS:, :COLS] = jnp.where(upper, low, high)
        fields[k, ROWS:, COLS:] = jnp.where(upper, below[part][:8], above[part][-8:])

    change = inverse_y(end_exchange(0), dft, turn_y)
    for p in range(2):
        normal[p] = change[p][:8]
        shear[p] = change[p][8:]

    def sweep(i, carry):
        stress = []
        for p in range(2):
            stress_normal, stress_shear, _ = local_stress(normal[p], shear[p], fraction_pencil[p])
            stress.append(jnp.concatenate([stress_normal, stress_shear], 0))
        start_exchange(2 * i + 1, forward_y(stress, dft, turn_y))
        arrived = end_exchange(2 * i + 1)
        start_exchange(2 * i + 2, spectral(arrived, dft, turn, small, green))
        change = inverse_y(end_exchange(2 * i + 2), dft, turn_y)
        for p in range(2):
            normal[p] += change[p][:8]
            shear[p] += change[p][8:]
        return carry

    lax.fori_loop(0, ITERS - 1, sweep, 0)

    energies = []
    for p in range(2):
        stress_normal, stress_shear, excess = local_stress(normal[p], shear[p], fraction_pencil[p])
        density = stress_normal * excess + 2.0 * stress_shear * shear[p]
        energies.append(0.5 * (density + pltpu.roll(density, 4, 0)))
    energy = jnp.where(upper_wide, energies[0], energies[1])
    shears = jnp.where(upper_wide, shear[0], pltpu.roll(shear[1], 4, 0))
    left = lax.broadcasted_iota(jnp.int32, (8, COLS), 1) < COLS // 2

    def block(values, g):
        return values[:, COLS * (g % GY) : COLS * (g % GY) + COLS]

    for g in range(GY):
        energy_sent[g, :, :COLS] = block(energy, g)
        energy_sent[g, :, COLS:] = jnp.where(left, block(energy, g + 1), block(energy, g - 1))

    def edge_copy(g, slot, there):
        return pltpu.make_async_remote_copy(
            energy_sent.at[g],
            energy_got.at[GY + slot],
            edge_send.at[slot],
            edge_recv.at[slot],
            device_id=(there, g),
            device_id_type=MESH,
        )

    @pl.when(gy == 0)
    def _():
        for g in range(GY):
            edge_copy(g, 0, down).start()

    @pl.when(gy == GY - 1)
    def _():
        for g in range(GY):
            edge_copy(g, 1, up).start()

    energy_copies = to_peers(energy_sent, energy_got, last_send.at[0], last_recv.at[0])
    for g in range(GY):
        strain_sent[g, 0:8] = block(normal[0], g)
        strain_sent[g, 8:16] = block(normal[1], g)
        strain_sent[g, 16:24] = block(shears, g)
    strain_copies = to_peers(strain_sent, strain_got, last_send.at[1], last_recv.at[1])
    energy_got[gy] = energy_sent[gy]
    strain_got[gy] = strain_sent[gy]

    total(first_sent, first_got, first_sem.at[0], first_sem.at[1], DEVICES - 1).wait_send()
    fraction_copies.wait_send()
    for copy in halos:
        copy.wait_send()
    for slot in range(2 * ITERS - 1):
        exchanged(slot).wait_send()

    energy_copies.wait_recv()
    for slot in range(2):
        edge_copy(0, slot, up).wait_recv()
    low = lax.broadcasted_iota(jnp.int32, (8, 2 * COLS), 0) < 4

    for layer in range(2):
        pieces = []
        for pair in range(GY // 2 + 1):
            one, two = energy_got[2 * pair], energy_got[2 * pair + 1]
            if layer == 0:
                pieces.append(jnp.where(low, one, pltpu.roll(two, 4, 0)))
            else:
                pieces.append(jnp.where(low, pltpu.roll(one, 4, 0), two))
        drive = fields[2 + layer] + elastic_weight * jnp.concatenate(pieces, 0) + base_rate
        sites = fields[layer]
        tall, wide = ROWS + 8, 2 * COLS
        for section in range(SECTIONS):
            way = fields[6 + 2 * section + layer]
            above, below = pltpu.roll(sites, 1, 0), pltpu.roll(sites, tall - 1, 0)
            ahead, behind = pltpu.roll(sites, wide - 1, 1), pltpu.roll(sites, 1, 1)
            neighbours = above + below + behind + ahead
            rate = 1.0 / (1.0 + jnp.exp(bond_energy * neighbours - drive))
            target = jnp.where(
                way == 0.0,
                below,
                jnp.where(way == 1.0, above, jnp.where(way == 2.0, ahead, behind)),
            )
            flux = jnp.where(
                fields[4 + layer] == float(section), rate * sites * (1.0 - target), 0.0
            )
            parted = [jnp.where(way == float(number), flux, 0.0) for number in range(4)]
            sites = (
                sites
                - flux
                + (
                    pltpu.roll(parted[0], 1, 0)
                    + pltpu.roll(parted[1], tall - 1, 0)
                    + pltpu.roll(parted[2], 1, 1)
                    + pltpu.roll(parted[3], wide - 1, 1)
                )
            )
        composition_out[layer] = sites[:ROWS, :COLS]

    strain_copies.wait_recv()
    for g in range(GY):
        rows = slice(4 * g, 4 * g + 4)
        for layer in range(2):
            strain_out[0, layer, rows] = strain_got[g, 8 * layer : 8 * layer + 4]
            strain_out[1, layer, rows] = strain_got[g, 8 * layer + 4 : 8 * layer + 8]
            strain_out[2, layer, rows] = strain_got[g, 16 + 4 * layer : 20 + 4 * layer]

    energy_copies.wait_send()
    strain_copies.wait_send()

    @pl.when(gy == 0)
    def _():
        for g in range(GY):
            edge_copy(g, 0, down).wait_send()

    @pl.when(gy == GY - 1)
    def _():
        for g in range(GY):
            edge_copy(g, 1, up).wait_send()


def on_device(occupancy, colour, hop_direction, barrier):
    operands = (occupancy, colour, hop_direction, barrier) + tuple(
        jnp.asarray(table) for table in tables()
    )
    vmem = pl.BlockSpec(memory_space=pltpu.VMEM)
    dma = pltpu.SemaphoreType.DMA
    exchanges = 2 * ITERS - 1
    return pl.pallas_call(
        kernel,
        out_shape=(
            jax.ShapeDtypeStruct((3, 2, ROWS, COLS), F32),
            jax.ShapeDtypeStruct((2, ROWS, COLS), F32),
        ),
        in_specs=[pl.BlockSpec(memory_space=pltpu.HBM)] * len(operands),
        out_specs=(vmem, vmem),
        scratch_shapes=[
            pltpu.VMEM((2, ROWS, COLS), jnp.int32),
            pltpu.VMEM((2, ROWS, COLS), jnp.int32),
            pltpu.VMEM((2, 2, ROWS, COLS), jnp.int32),
            pltpu.VMEM((2, ROWS, COLS), F32),
            pltpu.VMEM((1024, 512), BF16),
            pltpu.VMEM((128, 896), BF16),
            pltpu.VMEM((4, 256, 128), F32),
            pltpu.VMEM((2, 64, 256), F32),
            pltpu.VMEM((2, 16, COLS), F32),
            pltpu.VMEM((3, 256, 128), F32),
            pltpu.VMEM((2, 8, POINTS), F32),
            pltpu.VMEM((2, 8, POINTS), F32),
            pltpu.VMEM((2, 8, POINTS), F32),
            pltpu.VMEM((DEVICES, 2, 128), F32),
            pltpu.VMEM((DEVICES, 2, 128), F32),
            pltpu.VMEM((exchanges, DEVICES, 1, 128), F32),
            pltpu.VMEM((exchanges, DEVICES, 1, 128), F32),
            pltpu.VMEM((GY, 8, COLS), F32),
            pltpu.VMEM((GY, 8, COLS), F32),
            pltpu.VMEM((STATIC, ROWS, COLS), F32),
            pltpu.VMEM((2, STATIC // 2, 8, COLS), F32),
            pltpu.VMEM((2, STATIC // 2, 8, COLS), F32),
            pltpu.VMEM((2, 8, 384), F32),
            pltpu.VMEM((2, 8, 384), F32),
            pltpu.VMEM((4, 8, 384), F32),
            pltpu.VMEM((STATIC, ROWS + 8, 2 * COLS), F32),
            pltpu.VMEM((GY, 24, COLS), F32),
            pltpu.VMEM((GY, 24, COLS), F32),
            pltpu.VMEM((GY, 8, 2 * COLS), F32),
            pltpu.VMEM((GY + 2, 8, 2 * COLS), F32),
            dma((9,)),
            dma((2,)),
            dma((exchanges,)),
            dma((exchanges,)),
            dma((2,)),
            dma((8,)),
            dma((8,)),
            dma((2,)),
            dma((2,)),
            dma((2,)),
            dma((2,)),
        ],
        compiler_params=pltpu.CompilerParams(
            collective_id=0, has_side_effects=True, vmem_limit_bytes=62 * 1024 * 1024
        ),
        name="film",
    )(*operands)


def solution(mesh):
    placed = (
        P(None, "gx", "gy"),
        P(None, "gx", "gy"),
        P(None, None, "gx", "gy"),
        P(None, "gx", "gy"),
    )
    return jax.shard_map(
        on_device,
        mesh=mesh,
        in_specs=placed,
        out_specs=(P(None, None, "gx", "gy"), P(None, "gx", "gy")),
        check_vma=False,
    )
```

time: 92.6 us -> 77 us (0.83)
  local copies, waits for them, and re-layouts: 9.95 us -> 2.16 us
  Pallas kernels: 81.5 us -> 74.1 us
    unnamed x22 -> x4, local copies, waits for them, and re-layouts: 9.95 us -> 2.16 us
    pallas_call x1, Pallas kernels: 81.5 us -> 74.1 us  [on_device(): pl.pallas_call(kernel, out_shape=(jax.ShapeDtypeStruct((3, 2, ROWS, COLS)...]
where the time goes in v2:
time: 77 us; the launch traced here: 76.9 us
  Pallas kernels  74.1 us (96%)
  local copies, waits for them, and re-layouts  2.16 us (3%)
    pallas_call x1, Pallas kernels, on_device(): pl.pallas_call(kernel, out_shape=(jax.ShapeDtypeStruct((3, 2, ROWS, COLS)...  74.1 us
    unnamed x4, local copies, waits for them, and re-layouts  2.16 us

profile of v2, /device:TPU:1, one launch (start us, length us, event | category | flops | bytes accessed | tf_op | source)
XLA Modules:
  0.0 76.9 jit_solution(12802129098124513554)
XLA Ops:
  0.6 74.1 %film.1 = (f32[3,2,32,128]{3,2,1,0:T(8,128)}, f32[2,32,128]{2,1,0:T(8,128)}) custom-call(s32[2,32,128]{2,1,0:T(8,128)} %occupancy_in.1, s32[2,32,128]{2,1,0:T(8,128)} %colour_in.1, s32[2,2,32,128]{3,2,1,0:T(8,128)} %direction_in.1, f32[2,32,128]{2,1,0:T(8,128)} %barrier_in.1, bf16[1024,512]{1,0:T(8,128)(2,1)} %constant.10.clone.dft_in, ...), custom_call_target="tpu_custom_call" | custom-call | tf_op jit(solution)/shard_map/film/pallas_call | solution.py:673
  74.7 0.0 copy-start
  74.7 1.5 %copy.13 = f32[3,2,32,128]{3,2,1,0:T(8,128)} copy(f32[3,2,32,128]{3,2,1,0:T(8,128)} %get-tuple-element.4) | data formatting | bytes 196608
  76.3 0.0 copy-done
  76.3 0.6 copy.14
Async XLA Ops:
  74.7 1.6 %copy-start = (f32[2,32,128]{2,1,0:T(8,128)S(1)}, f32[2,32,128]{2,1,0:T(8,128)}, u32[]{:S(2)}) copy-start(f32[2,32,128]{2,1,0:T(8,128)} %get-tuple-element.5) | copy-start | bytes 98308

commit v3 on v2

--- a/solution.py
+++ b/solution.py
@@ -41,14 +41,22 @@
     return np.concatenate([np.cos(angle), np.sin(angle)], axis)
 
 
+def half_waves(angle):
+    return np.concatenate([np.cos(angle[:144]), np.sin(angle[:128])], 0)
+
+
 def tables():
     index = np.arange(256)
     angle = 2 * np.pi * (np.outer(index, index) % 256) / 256
     coarse = 2 * np.pi * (np.outer(index, index // 8) % 32) / 32
-    dft = split(waves(angle, 1)) + split(waves(coarse, 1))
+    order = np.concatenate([index[:129], 384 - index[129:]])
+    both = np.concatenate([np.cos(angle[order]), np.sin(angle[order])], 1)
+    back = np.concatenate([np.cos(angle[:, :128]), np.sin(angle[:, :128])], 1)
+    back[:, 128] = np.cos(angle[:, 128])
+    dft = split(half_waves(angle)) + split(half_waves(coarse)) + split(back)
     lane = np.arange(128)
-    turn_x = waves(2 * np.pi * np.outer(index, lane % 4) / POINTS, 0)
-    turn_first = waves(2 * np.pi * np.outer(index, lane // 16 * 4 + lane % 4) / POINTS, 0)
+    turn_x = waves(2 * np.pi * np.outer(order, lane % 4) / POINTS, 0)
+    turn_first = waves(2 * np.pi * np.outer(order, lane // 16 * 4 + lane % 4) / POINTS, 0)
     turn_y = waves(2 * np.pi * np.outer(np.arange(64) // 16, index) / POINTS, 0).reshape(2, 64, 256)
     stress = -2.0 * (lame_germanium + shear_germanium)
     angle = 2 * np.pi * np.outer(np.arange(16) // 4, np.arange(POINTS)) / POINTS
@@ -72,9 +80,11 @@
     for p in range(2):
         for n in range(128):
             picked[p * 128 + n] = first4[p * 64 + n // 4 % 4 * 16 + n % 4]
+    both = np.concatenate(split(both), 0)
     small = np.concatenate([forward4, inverse4, picked[:128], picked[128:]], 1)
     return (
         np.concatenate(dft, 0),
+        both,
         small.astype(ml_dtypes.bfloat16),
         np.concatenate([turn_x, turn_first], 0).reshape(4, 256, 128).astype(np.float32),
         turn_y.astype(np.float32),
@@ -91,16 +101,30 @@
     return lax.dot_general(left, right, (dims, ((), ())), preferred_element_type=F32)
 
 
-def table_left(dft, values):
+def wide(table, values, dims):
     high, low = halves(values)
-    wide = dot(dft[0][...], jnp.concatenate([high, low], 1), ((1,), (0,)))
-    return wide[:, :128] + wide[:, 128:] + dot(dft[1][...], high, ((1,), (0,)))
-
-
-def table_left_turned(dft, rows):
-    high, low = halves(rows)
-    wide = dot(dft[0][...], jnp.concatenate([high, low], 0), ((1,), (1,)))
-    return wide[:, :128] + wide[:, 128:] + dot(dft[1][...], high, ((1,), (1,)))
+    both = dot(table[0][...], jnp.concatenate([high, low], 1 - dims[1][0]), dims)
+    return both[:, :128] + both[:, 128:] + dot(table[1][...], high, dims)
+
+
+def narrow(table, values, dims):
+    return three([part[...] for part in table], halves(values), dims)
+
+
+def parity(dft, multiply, plain, crossed, dims):
+    even, odd = multiply(dft[0], plain, dims), multiply(dft[1], crossed, dims)
+    minus = even[:128] - odd
+    return jnp.concatenate(
+        [even[:128] + odd, first_row(even[128:136], minus[:8]), minus[8:]], 0
+    )
+
+
+def first_row(special, others):
+    return jnp.where(lax.broadcasted_iota(jnp.int32, others.shape, 0) == 0, special, others)
+
+
+def folded(values):
+    return values[:128] + values[128:], values[:128] - values[128:]
 
 
 def three(left, right, dims):
@@ -115,8 +139,9 @@
     shape = (256, 128)
     lane = lax.broadcasted_iota(jnp.int32, shape, 1)
     comp = lax.rem(lane // 4, 4)
-    index_x = lax.broadcasted_iota(jnp.int32, shape, 0) + 256 * lax.rem(lane, 4)
-    index_y = 4 * device + lax.rem(lane // 16, 4)
+    row = lax.broadcasted_iota(jnp.int32, shape, 0)
+    index_x = jnp.where(row > 128, 384 - row, row) + 256 * lax.rem(lane, 4)
+    index_y = 4 * jnp.where(device > 128, 384 - device, device) + lax.rem(lane // 16, 4)
     unit = 2.0 * math.pi / POINTS
     a = jnp.where(index_x < POINTS // 2, index_x, index_x - POINTS).astype(F32) * unit
     b = jnp.where(index_y < POINTS // 2, index_y, index_y - POINTS).astype(F32) * unit
@@ -150,39 +175,39 @@
     return jnp.where(lax.broadcasted_iota(jnp.int32, shape, 1) < 64, 1.0, -1.0)
 
 
-def spectral(received, dft, turn, small, green):
+def spectral(received, dft, back, turn, small, green):
     sign = crossing((256, 128))
     swapped = pltpu.roll(received, 64, 1) * sign
-    first = table_left(dft, jnp.concatenate([received, swapped], 0))
+    first = wide(dft, jnp.concatenate([received, swapped], 0), ((1,), (0,)))
     turned = turn[0] * first + turn[1] * (pltpu.roll(first, 64, 1) * sign)
     spread = exact(turned, small[:, :384])
     mapped = (
         green[0] * spread[:, :128] + green[1] * spread[:, 128:256] + green[2] * spread[:, 256:]
     )
-    return spectral_back(mapped, dft, turn, small)
-
-
-def spectral_back(mapped, dft, turn, small):
-    back = exact(mapped, small[:, 384:640])
-    plain, crossed = back[:, :128], back[:, 128:]
+    return spectral_back(mapped, back, turn, small)
+
+
+def spectral_back(mapped, back, turn, small):
+    both = exact(mapped, small[:, 384:640])
+    plain, crossed = both[:, :128], both[:, 128:]
     values = turn[0] * plain + turn[1] * crossed
     crossed = turn[0] * crossed - turn[1] * plain
-    return table_left(dft, jnp.concatenate([values, crossed], 0))
-
-
-def spectral_first(received, dft, coarse, turn, small, green):
+    even, odd = folded(values)[0], folded(crossed)[1]
+    even = [first_row(values[:8], even[:8]), even[8:]]
+    odd = [first_row(values[128:136], odd[:8]), odd[8:]]
+    return wide(back, jnp.concatenate(even + odd, 0), ((1,), (0,)))
+
+
+def spectral_first(received, coarse, back, turn, small, green):
     real, imag = received[:, :128], received[:, 128:]
-    both = jnp.concatenate(
-        [jnp.concatenate([real, imag], 1), jnp.concatenate([imag, -real], 1)], 0
-    )
-    first = three([part[...] for part in coarse], halves(both), ((1,), (0,)))
+    first = parity(coarse, narrow, received, jnp.concatenate([imag, -real], 1), ((1,), (0,)))
     real, imag = first[:, :128], first[:, 128:]
     real, imag = turn[2] * real + turn[3] * imag, turn[2] * imag - turn[3] * real
     spread = exact(
         jnp.concatenate([real, imag], 1),
         jnp.concatenate([small[:, 640:768], small[:, 768:896]], 0),
     )
-    return spectral_back((green[0] + green[1]) * spread, dft, turn, small)
+    return spectral_back((green[0] + green[1]) * spread, back, turn, small)
 
 
 def first_y(fields, dft, turn, odd):
@@ -199,11 +224,9 @@
     real, imag = spread
     cos, sin = (jnp.concatenate([turn[k]] * 8, 0) for k in range(2))
     real, imag = cos * real + sin * imag, cos * imag - sin * real
-    rows = jnp.concatenate(
-        [jnp.concatenate([real, imag], 1), jnp.concatenate([imag, -real], 1)], 0
-    )
-    table = [jnp.concatenate([part[:, :128], part[:, 256:384]], 1) for part in dft]
-    out = three(table, halves(rows), ((1,), (1,)))
+    plain, crossed = jnp.concatenate([real, imag], 0), jnp.concatenate([imag, -real], 0)
+    table = [[part.at[:, pl.ds(0, 128)] for part in parts] for parts in dft]
+    out = parity(table, narrow, plain, crossed, ((1,), (1,)))
     flip = lax.rem(lax.broadcasted_iota(jnp.int32, out.shape, 0), 2) * odd
     return out * (1 - 2 * flip).astype(F32)
 
@@ -224,23 +247,20 @@
     real, imag = (jnp.concatenate(list(part), 0) for part in four(parts, -1))
     turned_real = turn_y[0] * real + turn_y[1] * imag
     turned_imag = turn_y[0] * imag - turn_y[1] * real
-    rows = jnp.concatenate(
-        [
-            jnp.concatenate([turned_real, turned_imag], 1),
-            jnp.concatenate([turned_imag, -turned_real], 1),
-        ],
-        0,
-    )
-    return table_left_turned(dft, rows)
-
-
-def inverse_y(received, dft, turn_y):
-    across = received.T
-    real, imag = across[:64], across[64:]
-    rows = jnp.concatenate(
-        [jnp.concatenate([real, -imag], 1), jnp.concatenate([imag, real], 1)], 0
-    )
-    both = three(halves(rows), [part[...] for part in dft], ((1,), (1,)))
+    plain = jnp.concatenate([turned_real, turned_imag], 0)
+    crossed = jnp.concatenate([turned_imag, -turned_real], 0)
+    return parity(dft, wide, plain, crossed, ((1,), (1,)))
+
+
+def inverse_y(received, back, turn_y):
+    even, odd = folded(received)
+    highest = pltpu.roll(received[128:136], 64, 1) * crossing((8, 128))
+    even = [first_row(received[:8], even[:8]), even[8:]]
+    odd = [first_row(highest, odd[:8]), odd[8:]]
+    across = jnp.concatenate(even + odd, 0).T
+    odd = jnp.concatenate([-across[64:, 128:], across[:64, 128:]], 0)
+    rows = jnp.concatenate([across[:, :128], odd], 1)
+    both = three(halves(rows), [part[...] for part in back], ((1,), (1,)))
     real, imag = both[:64], both[64:]
     turned_real = turn_y[0] * real - turn_y[1] * imag
     turned_imag = turn_y[0] * imag + turn_y[1] * real
@@ -258,6 +278,14 @@
     return lame_field * trace + shear_field * excess, shear_field * shear, excess
 
 
+def dft_parts(dfts):
+    dft, coarse = (
+        [[dfts.at[pl.ds(at + 272 * k + start, size)] for k in range(2)] for start, size in ((0, 144), (144, 128))]
+        for at in (0, 544)
+    )
+    return dft, coarse, [dfts.at[pl.ds(1088 + 256 * k, 256)] for k in range(2)]
+
+
 def ring(steps, size):
     return min(steps % size, -steps % size)
 
@@ -268,6 +296,7 @@
     direction_in,
     barrier_in,
     dft_in,
+    both_in,
     small_in,
     turn_in,
     turn_y_in,
@@ -279,6 +308,7 @@
     direction,
     barrier,
     dfts,
+    both,
     small,
     turn,
     turn_y,
@@ -331,6 +361,7 @@
         (small_in, small),
         (turn_in, turn),
         (turn_y_in, turn_y),
+        (both_in, both),
     ]
     inputs = [
         pltpu.make_async_copy(source, target, input_sem.at[k])
@@ -367,8 +398,8 @@
         )
     )
 
-    dft = (dfts.at[pl.ds(0, 256)], dfts.at[pl.ds(256, 256)])
-    coarse = (dfts.at[pl.ds(512, 256)], dfts.at[pl.ds(768, 256)])
+    dft, coarse, back = dft_parts(dfts)
+    whole = [both.at[pl.ds(256 * k, 256)] for k in range(2)]
 
     for copy in inputs[:3]:
         copy.wait()
@@ -494,7 +525,7 @@
         exchanged(slot).wait_recv()
         return landed[slot, :, 0, :]
 
-    start_exchange(0, spectral_first(received, dft, coarse, turn, small, green))
+    start_exchange(0, spectral_first(received, coarse, back, turn, small, green))
 
     fraction_copies.wait_recv()
     pencil = jnp.concatenate([fraction_got[g] for g in range(GY)], 1)
@@ -525,7 +556,7 @@
         fields[k, ROWS:, :COLS] = jnp.where(upper, low, high)
         fields[k, ROWS:, COLS:] = jnp.where(upper, below[part][:8], above[part][-8:])
 
-    change = inverse_y(end_exchange(0), dft, turn_y)
+    change = inverse_y(end_exchange(0), back, turn_y)
     for p in range(2):
         normal[p] = change[p][:8]
         shear[p] = change[p][8:]
@@ -537,8 +568,8 @@
             stress.append(jnp.concatenate([stress_normal, stress_shear], 0))
         start_exchange(2 * i + 1, forward_y(stress, dft, turn_y))
         arrived = end_exchange(2 * i + 1)
-        start_exchange(2 * i + 2, spectral(arrived, dft, turn, small, green))
-        change = inverse_y(end_exchange(2 * i + 2), dft, turn_y)
+        start_exchange(2 * i + 2, spectral(arrived, whole, back, turn, small, green))
+        change = inverse_y(end_exchange(2 * i + 2), back, turn_y)
         for p in range(2):
             normal[p] += change[p][:8]
             shear[p] += change[p][8:]
@@ -683,7 +714,8 @@
             pltpu.VMEM((2, ROWS, COLS), jnp.int32),
             pltpu.VMEM((2, 2, ROWS, COLS), jnp.int32),
             pltpu.VMEM((2, ROWS, COLS), F32),
-            pltpu.VMEM((1024, 512), BF16),
+            pltpu.VMEM((1600, 256), BF16),
+            pltpu.VMEM((512, 512), BF16),
             pltpu.VMEM((128, 896), BF16),
             pltpu.VMEM((4, 256, 128), F32),
             pltpu.VMEM((2, 64, 256), F32),
@@ -709,7 +741,7 @@
             pltpu.VMEM((GY, 24, COLS), F32),
             pltpu.VMEM((GY, 8, 2 * COLS), F32),
             pltpu.VMEM((GY + 2, 8, 2 * COLS), F32),
-            dma((9,)),
+            dma((10,)),
             dma((2,)),
             dma((exchanges,)),
             dma((exchanges,)),
@@ -722,10 +754,10 @@
             dma((2,)),
         ],
         compiler_params=pltpu.CompilerParams(
-            collective_id=0, has_side_effects=True, vmem_limit_bytes=62 * 1024 * 1024
+            collective_id=0, has_side_effects=True, vmem_limit_bytes=40 * 1024 * 1024
         ),
         name="film",
-    )(*operands)
+    )(*[pltpu.with_memory_space_constraint(x, pltpu.HBM) for x in operands])
 
 
 def solution(mesh):

time: 77 us -> 74.2 us (0.964)
  Pallas kernels: 74.1 us -> 72.3 us
  local copies, waits for them, and re-layouts: 2.16 us -> 1.26 us
    pallas_call x1, Pallas kernels: 74.1 us -> 72.3 us  [on_device(): pl.pallas_call(kernel, out_shape=(jax.ShapeDtypeStruct((3, 2, ROWS, COLS)...]
    unnamed x4 -> x2, local copies, waits for them, and re-layouts: 2.16 us -> 1.26 us
where the time goes in v3:
time: 74.2 us
  Pallas kernels  72.3 us (97%)
  local copies, waits for them, and re-layouts  1.26 us (2%)
    pallas_call x1, Pallas kernels, on_device(): pl.pallas_call(kernel, out_shape=(jax.ShapeDtypeStruct((3, 2, ROWS, COLS)...  72.3 us

profile of v3, /device:TPU:1, one launch (start us, length us, event | category | flops | bytes accessed | tf_op | source)
XLA Modules:
  0.0 74.2 jit_solution(748168430772742873)
XLA Ops:
  0.6 72.3 %film.1 = (f32[3,2,32,128]{3,2,1,0:T(8,128)S(1)}, f32[2,32,128]{2,1,0:T(8,128)S(1)}) custom-call(s32[2,32,128]{2,1,0:T(8,128)} %occupancy_in.1, s32[2,32,128]{2,1,0:T(8,128)} %colour_in.1, s32[2,2,32,128]{3,2,1,0:T(8,128)} %direction_in.1, f32[2,32,128]{2,1,0:T(8,128)} %barrier_in.1, bf16[1600,256]{1,0:T(8,128)(2,1)} %constant.12.clone.dft_in, ...), custom_call_target="tpu_custom_call" | custom-call | tf_op jit(solution)/shard_map/film/pallas_call | solution.py:704
  72.9 0.6 copy.14
  73.6 0.6 copy.15

commit v4 on v3

--- a/solution.py
+++ b/solution.py
@@ -1,3 +1,4 @@
+import functools
 import math
 
 import jax
@@ -48,12 +49,13 @@
 def tables():
     index = np.arange(256)
     angle = 2 * np.pi * (np.outer(index, index) % 256) / 256
-    coarse = 2 * np.pi * (np.outer(index, index // 8) % 32) / 32
+    coarse = np.concatenate([index[:32], -index[:32] % 32])
+    coarse = 2 * np.pi * (np.outer(coarse, index // 8) % 32) / 32
     order = np.concatenate([index[:129], 384 - index[129:]])
     both = np.concatenate([np.cos(angle[order]), np.sin(angle[order])], 1)
     back = np.concatenate([np.cos(angle[:, :128]), np.sin(angle[:, :128])], 1)
     back[:, 128] = np.cos(angle[:, 128])
-    dft = split(half_waves(angle)) + split(half_waves(coarse)) + split(back)
+    dft = split(half_waves(angle)) + split(waves(coarse, 0)) + split(back)
     lane = np.arange(128)
     turn_x = waves(2 * np.pi * np.outer(order, lane % 4) / POINTS, 0)
     turn_first = waves(2 * np.pi * np.outer(order, lane // 16 * 4 + lane % 4) / POINTS, 0)
@@ -199,9 +201,12 @@
 
 
 def spectral_first(received, coarse, back, turn, small, green):
-    real, imag = received[:, :128], received[:, 128:]
-    first = parity(coarse, narrow, received, jnp.concatenate([imag, -real], 1), ((1,), (0,)))
-    real, imag = first[:, :128], first[:, 128:]
+    both = three([part[...] for part in coarse], halves(received), ((1,), (0,)))
+    cos, sin = both[:64], both[64:]
+    real, imag = (
+        jnp.concatenate([part[:32]] * 4 + [part[32:]] * 4, 0)
+        for part in (cos[:, :128] + sin[:, 128:], cos[:, 128:] - sin[:, :128])
+    )
     real, imag = turn[2] * real + turn[3] * imag, turn[2] * imag - turn[3] * real
     spread = exact(
         jnp.concatenate([real, imag], 1),
@@ -279,11 +284,10 @@
 
 
 def dft_parts(dfts):
-    dft, coarse = (
-        [[dfts.at[pl.ds(at + 272 * k + start, size)] for k in range(2)] for start, size in ((0, 144), (144, 128))]
-        for at in (0, 544)
-    )
-    return dft, coarse, [dfts.at[pl.ds(1088 + 256 * k, 256)] for k in range(2)]
+    def rows(at, step, size):
+        return [dfts.at[pl.ds(at + step * k, size)] for k in range(2)]
+
+    return [rows(0, 272, 144), rows(144, 272, 128)], rows(544, 128, 128), rows(800, 256, 256)
 
 
 def ring(steps, size):
@@ -367,29 +371,38 @@
         pltpu.make_async_copy(source, target, input_sem.at[k])
         for k, (source, target) in enumerate(inputs)
     ]
-    for copy in inputs:
-        copy.start()
-
-    places = sorted(
-        [(dx, dy, dc) for dx in range(4) for dy in range(4) for dc in range(2)],
-        key=lambda t: -(ring(t[0], 4) + ring(t[1], 4) + 0.5 * t[2]),
-    )
-    bases = []
-    for dx, dy, dc in places:
-        x_there, y_there, c_there = lax.rem(x + dx, 4), lax.rem(y + dy, 4), lax.rem(core + dc, 2)
-        bases.append((lax.rem(y_there, 2) * 16 + c_there, x_there * 2 + y_there // 2))
+    x_part = [lax.rem(x + dx, 4) * 2 for dx in range(4)]
+    y_part = [lax.rem(y + dy, 4) for dy in range(4)]
+    y_part = [(lax.rem(there, 2) * 16, there // 2) for there in y_part]
+    c_part = [core, 1 - core]
+    groups = [[] for _ in range(5)]
+    for dx in range(4):
+        for dy in range(4):
+            for dc in (1, 0):
+                there = (y_part[dy][0] + c_part[dc], x_part[dx] + y_part[dy][1])
+                groups[ring(dx, 4) + ring(dy, 4)].append(there)
 
     def to_others(send):
+        def at(z_there, places):
+            for gx_part, gy_there in places:
+                send(gx_part + 2 * z_there, gy_there)
+
         def step(i, carry):
-            steps = jnp.where(lax.rem(i, 2) == 0, 4 + i // 2, 4 - (i + 1) // 2)
-            z_there = lax.rem(z + steps, 8)
-            for base_x, base_y in bases:
-                send(base_x + 2 * z_there, base_y)
+            for hops in (4, 3, 2, 1, 0):
+                along_z = 8 - i - hops
+                up_z, down_z = lax.rem(z + along_z + 8, 8), lax.rem(z - along_z + 8, 8)
+                within = (along_z >= 0) & (along_z <= 4)
+                if hops > 0:
+                    pl.when(within)(functools.partial(at, up_z, groups[hops]))
+                else:
+                    pl.when(within)(functools.partial(at, up_z, groups[0][:1]))
+                    pl.when((along_z >= 1) & within)(functools.partial(at, up_z, groups[0][1:]))
+                pl.when((along_z >= 1) & (along_z <= 3))(
+                    functools.partial(at, down_z, groups[hops])
+                )
             return carry
 
-        lax.fori_loop(0, 7, step, 0)
-        for base_x, base_y in bases[:-1]:
-            send(base_x + 2 * z, base_y)
+        lax.fori_loop(0, 9, step, 0)
 
     entry = pltpu.get_barrier_semaphore()
     to_others(
@@ -397,6 +410,9 @@
             entry, inc=1, device_id=(there_x, there_y), device_id_type=MESH
         )
     )
+
+    for copy in inputs:
+        copy.start()
 
     dft, coarse, back = dft_parts(dfts)
     whole = [both.at[pl.ds(256 * k, 256)] for k in range(2)]
@@ -629,10 +645,44 @@
     for slot in range(2 * ITERS - 1):
         exchanged(slot).wait_send()
 
+    low = lax.broadcasted_iota(jnp.int32, (8, 2 * COLS), 0) < 4
+    tall, wide_cols = ROWS + 8, 2 * COLS
+
+    def prepared(sites, layer, section):
+        way = fields[6 + 2 * section + layer]
+        above, below = pltpu.roll(sites, 1, 0), pltpu.roll(sites, tall - 1, 0)
+        ahead, behind = pltpu.roll(sites, wide_cols - 1, 1), pltpu.roll(sites, 1, 1)
+        neighbours = above + below + behind + ahead
+        target = jnp.where(
+            way == 0.0,
+            below,
+            jnp.where(way == 1.0, above, jnp.where(way == 2.0, ahead, behind)),
+        )
+        moving = jnp.where(
+            fields[4 + layer] == float(section), sites * (1.0 - target), 0.0
+        )
+        return bond_energy * neighbours - (fields[2 + layer] + base_rate), moving
+
+    def hop(sites, ready, energy, layer, section):
+        flux = ready[1] / (1.0 + jnp.exp(ready[0] - elastic_weight * energy))
+        way = fields[6 + 2 * section + layer]
+        parted = [jnp.where(way == float(number), flux, 0.0) for number in range(4)]
+        return (
+            sites
+            - flux
+            + (
+                pltpu.roll(parted[0], 1, 0)
+                + pltpu.roll(parted[1], tall - 1, 0)
+                + pltpu.roll(parted[2], 1, 1)
+                + pltpu.roll(parted[3], wide_cols - 1, 1)
+            )
+        )
+
+    ready = [prepared(fields[layer], layer, 0) for layer in range(2)]
+
     energy_copies.wait_recv()
     for slot in range(2):
         edge_copy(0, slot, up).wait_recv()
-    low = lax.broadcasted_iota(jnp.int32, (8, 2 * COLS), 0) < 4
 
     for layer in range(2):
         pieces = []
@@ -642,34 +692,10 @@
                 pieces.append(jnp.where(low, one, pltpu.roll(two, 4, 0)))
             else:
                 pieces.append(jnp.where(low, pltpu.roll(one, 4, 0), two))
-        drive = fields[2 + layer] + elastic_weight * jnp.concatenate(pieces, 0) + base_rate
-        sites = fields[layer]
-        tall, wide = ROWS + 8, 2 * COLS
-        for section in range(SECTIONS):
-            way = fields[6 + 2 * section + layer]
-            above, below = pltpu.roll(sites, 1, 0), pltpu.roll(sites, tall - 1, 0)
-            ahead, behind = pltpu.roll(sites, wide - 1, 1), pltpu.roll(sites, 1, 1)
-            neighbours = above + below + behind + ahead
-            rate = 1.0 / (1.0 + jnp.exp(bond_energy * neighbours - drive))
-            target = jnp.where(
-                way == 0.0,
-                below,
-                jnp.where(way == 1.0, above, jnp.where(way == 2.0, ahead, behind)),
-            )
-            flux = jnp.where(
-                fields[4 + layer] == float(section), rate * sites * (1.0 - target), 0.0
-            )
-            parted = [jnp.where(way == float(number), flux, 0.0) for number in range(4)]
-            sites = (
-                sites
-                - flux
-                + (
-                    pltpu.roll(parted[0], 1, 0)
-                    + pltpu.roll(parted[1], tall - 1, 0)
-                    + pltpu.roll(parted[2], 1, 1)
-                    + pltpu.roll(parted[3], wide - 1, 1)
-                )
-            )
+        energy_here = jnp.concatenate(pieces, 0)
+        sites = hop(fields[layer], ready[layer], energy_here, layer, 0)
+        for section in range(1, SECTIONS):
+            sites = hop(sites, prepared(sites, layer, section), energy_here, layer, section)
         composition_out[layer] = sites[:ROWS, :COLS]
 
     strain_copies.wait_recv()
@@ -714,7 +740,7 @@
             pltpu.VMEM((2, ROWS, COLS), jnp.int32),
             pltpu.VMEM((2, 2, ROWS, COLS), jnp.int32),
             pltpu.VMEM((2, ROWS, COLS), F32),
-            pltpu.VMEM((1600, 256), BF16),
+            pltpu.VMEM((1312, 256), BF16),
             pltpu.VMEM((512, 512), BF16),
             pltpu.VMEM((128, 896), BF16),
             pltpu.VMEM((4, 256, 128), F32),

time: 74.2 us -> 73.5 us (level)
  Pallas kernels: 72.3 us -> 71.5 us
where the time goes in v4:
time: 73.5 us; the launch traced here: 73.4 us
  Pallas kernels  71.5 us (97%)
  local copies, waits for them, and re-layouts  1.26 us (2%)
    pallas_call x1, Pallas kernels, on_device(): pl.pallas_call(kernel, out_shape=(jax.ShapeDtypeStruct((3, 2, ROWS, COLS)...  71.5 us

profile of v4, /device:TPU:1, one launch (start us, length us, event | category | flops | bytes accessed | tf_op | source)
XLA Modules:
  0.0 73.4 jit_solution(17229737084164714236)
XLA Ops:
  0.6 71.5 %film.1 = (f32[3,2,32,128]{3,2,1,0:T(8,128)S(1)}, f32[2,32,128]{2,1,0:T(8,128)S(1)}) custom-call(s32[2,32,128]{2,1,0:T(8,128)} %occupancy_in.1, s32[2,32,128]{2,1,0:T(8,128)} %colour_in.1, s32[2,2,32,128]{3,2,1,0:T(8,128)} %direction_in.1, f32[2,32,128]{2,1,0:T(8,128)} %barrier_in.1, bf16[1312,256]{1,0:T(8,128)(2,1)} %constant.12.clone.dft_in, ...), custom_call_target="tpu_custom_call" | custom-call | tf_op jit(solution)/shard_map/film/pallas_call | solution.py:730
  72.2 0.6 copy.14
  72.8 0.6 copy.15

commit v5 on v4

--- a/solution.py
+++ b/solution.py
@@ -405,11 +405,22 @@
         lax.fori_loop(0, 9, step, 0)
 
     entry = pltpu.get_barrier_semaphore()
-    to_others(
-        lambda there_x, there_y: pl.semaphore_signal(
-            entry, inc=1, device_id=(there_x, there_y), device_id_type=MESH
-        )
-    )
+    flat = [place for hops in (4, 3, 2, 1, 0) for place in groups[hops]]
+    flat = flat[:-2] + [groups[0][0], groups[0][1]]
+
+    def greet(z_there, places):
+        for gx_part, gy_there in places:
+            pl.semaphore_signal(
+                entry, inc=1, device_id=(gx_part + 2 * z_there, gy_there), device_id_type=MESH
+            )
+
+    def greet_step(i, carry):
+        steps = jnp.where(lax.rem(i, 2) == 0, 4 + i // 2, 4 - (i + 1) // 2)
+        greet(lax.rem(z + steps, 8), flat)
+        return carry
+
+    lax.fori_loop(0, 7, greet_step, 0)
+    greet(z, flat[:-1])
 
     for copy in inputs:
         copy.start()

time: 73.5 us -> 73.5 us (level)
  no operation moved by 1% of the time
where the time goes in v5:
time: 73.5 us; the launch traced here: 73.4 us
  Pallas kernels  71.5 us (97%)
  local copies, waits for them, and re-layouts  1.26 us (2%)
    pallas_call x1, Pallas kernels, on_device(): pl.pallas_call(kernel, out_shape=(jax.ShapeDtypeStruct((3, 2, ROWS, COLS)...  71.5 us

profile of v5, /device:TPU:1, one launch (start us, length us, event | category | flops | bytes accessed | tf_op | source)
XLA Modules:
  0.0 73.4 jit_solution(18161147044410771697)
XLA Ops:
  0.6 71.5 %film.1 = (f32[3,2,32,128]{3,2,1,0:T(8,128)S(1)}, f32[2,32,128]{2,1,0:T(8,128)S(1)}) custom-call(s32[2,32,128]{2,1,0:T(8,128)} %occupancy_in.1, s32[2,32,128]{2,1,0:T(8,128)} %colour_in.1, s32[2,2,32,128]{3,2,1,0:T(8,128)} %direction_in.1, f32[2,32,128]{2,1,0:T(8,128)} %barrier_in.1, bf16[1312,256]{1,0:T(8,128)(2,1)} %constant.12.clone.dft_in, ...), custom_call_target="tpu_custom_call" | custom-call | tf_op jit(solution)/shard_map/film/pallas_call | solution.py:741
  72.1 0.6 copy.14
  72.8 0.6 copy.15

commit v6 on v4

--- a/solution.py
+++ b/solution.py
@@ -591,7 +591,8 @@
             shear[p] += change[p][8:]
         return carry
 
-    lax.fori_loop(0, ITERS - 1, sweep, 0)
+    for i in range(ITERS - 1):
+        sweep(i, 0)
 
     energies = []
     for p in range(2):

time: 73.5 us -> 73.5 us (level)
  no operation moved by 1% of the time
where the time goes in v6:
time: 73.5 us; the launch traced here: 73.3 us
  Pallas kernels  71.5 us (97%)
  local copies, waits for them, and re-layouts  1.26 us (2%)
    pallas_call x1, Pallas kernels, on_device(): pl.pallas_call(kernel, out_shape=(jax.ShapeDtypeStruct((3, 2, ROWS, COLS)...  71.5 us

profile of v6, /device:TPU:1, one launch (start us, length us, event | category | flops | bytes accessed | tf_op | source)
XLA Modules:
  0.0 73.3 jit_solution(4436036632331733553)
XLA Ops:
  0.6 71.5 %film.1 = (f32[3,2,32,128]{3,2,1,0:T(8,128)S(1)}, f32[2,32,128]{2,1,0:T(8,128)S(1)}) custom-call(s32[2,32,128]{2,1,0:T(8,128)} %occupancy_in.1, s32[2,32,128]{2,1,0:T(8,128)} %colour_in.1, s32[2,2,32,128]{3,2,1,0:T(8,128)} %direction_in.1, f32[2,32,128]{2,1,0:T(8,128)} %barrier_in.1, bf16[1312,256]{1,0:T(8,128)(2,1)} %constant.12.clone.dft_in, ...), custom_call_target="tpu_custom_call" | custom-call | tf_op jit(solution)/shard_map/film/pallas_call | solution.py:731
  72.1 0.6 copy.14
  72.7 0.6 copy.15
